TPU v7x, 512 devices: a whole 4x4x16 slice. The times are simulated.
512 devices in a mesh: group: 4 (over x_hi, core), ans: 32 (over x_lo, z), tp: 4 (over y).
Axes of the slice: x: 4 (x_hi: 2, x_lo: 2; x = x_hi * 2 + x_lo), y: 4, z: 16, core: 2. Of those that a mesh axis runs over, the one named last changes fastest.
Arguments:
- q_ans: bfloat16 [16384, 4096], P(('group', 'ans'), 'tp'), parts along dimension 0, may hold values from -160 to 160
- kv_ans: bfloat16 [2, 16384, 512], P(None, ('group', 'ans'), 'tp'), parts along dimension 1, may hold values from -6 to 6
- q_prompt: bfloat16 [8192, 4096], P(('group', 'ans'), 'tp'), parts along dimension 0, may hold values from -160 to 160
- kv_prompt: bfloat16 [2, 8192, 512], P(None, ('group', 'ans'), 'tp'), parts along dimension 1, may hold values from -8 to 8
- dout_ans: bfloat16 [16384, 4096], P(('group', 'ans'), 'tp'), parts along dimension 0, may hold values from -48 to 48
- dout_prompt: bfloat16 [8192, 4096], P(('group', 'ans'), 'tp'), parts along dimension 0, may hold values from -48 to 48
- ans_len: int32 [128], P(('group', 'ans')), parts along dimension 0, may hold values from 32 to 128, as said below
- prompt_len: int32 [4], P('group'), parts along dimension 0, may hold values from 512 to 2048
Outputs:
- d_q_ans: bfloat16 [16384, 4096], P(('group', 'ans'), 'tp'), parts along dimension 0
- d_kv_ans: bfloat16 [2, 16384, 512], P(None, ('group', 'ans'), 'tp'), parts along dimension 1
- d_q_prompt: bfloat16 [8192, 4096], P(('group', 'ans'), 'tp'), parts along dimension 0
- d_kv_prompt: bfloat16 [2, 8192, 512], P(None, ('group', 'ans'), 'tp'), parts along dimension 1
There are 4 independent parts, one for each index of `group`. A program takes and returns all parts, laid end to end along the dimension named above; each array names one. Nothing has to cross between parts.
Inputs may be any that keep to these rules, and one draw needn't show every extreme that they name: `ans_len`: in every draw some answer has length 128.
All inputs are finite; a program needn't handle non-finite values.
Results may differ from a plain program's by a relative error of at most 0.015.
Values may be sent and summed in bfloat16 or wider, within the bound.
A program may use at most 128 MiB of HBM per device.

v0:
```python
import math

import jax
import jax.numpy as jnp
from jax import lax
from jax.sharding import PartitionSpec as P

HQ = 32
KVH = 4
HD = 128


NEG_FILL = -1e30


def scores_of(rows, keys, mask, scale):
    raw = jnp.einsum("nd,sd->ns", rows, keys, preferred_element_type=jnp.float32) * scale
    return jnp.where(mask, raw, NEG_FILL)


def block_pass(rows, grads_in, keys, values, mask, scale):
    score = scores_of(rows, keys, mask, scale)
    top = jnp.max(score, axis=1, keepdims=True)
    expo = jnp.exp(score - top)
    total = jnp.sum(expo, axis=1, keepdims=True)
    prob = expo / total
    prob_b = prob.astype(jnp.bfloat16)
    attended = jnp.dot(prob_b, values, preferred_element_type=jnp.float32)
    delta = jnp.sum(grads_in.astype(jnp.float32) * attended, axis=1, keepdims=True)
    dprob = jnp.einsum("nd,sd->ns", grads_in, values, preferred_element_type=jnp.float32)
    dscore = (prob * (dprob - delta) * scale).astype(jnp.bfloat16)
    dquery = jnp.dot(dscore, keys, preferred_element_type=jnp.float32)
    return (prob_b, dscore, dquery, top, total, delta)


def key_grads(prob_b, dscore, rows, grads_in):
    dkey = jnp.einsum("ns,nd->sd", dscore, rows, preferred_element_type=jnp.float32)
    dvalue = jnp.einsum("ns,nd->sd", prob_b, grads_in, preferred_element_type=jnp.float32)
    return (dkey, dvalue)


def prompt_mask(columns, limit, plen):
    return (columns[None, :] < plen) & (columns[None, :] <= limit[:, None])


def per_device(q_ans, kv_ans, q_prompt, kv_prompt, dout_ans, dout_prompt, ans_len, prompt_len):
    alen = q_ans.shape[0]
    piece = q_prompt.shape[0]
    group = HQ // KVH
    scale = 1.0 / math.sqrt(HD)
    gathered = lax.all_gather(kv_prompt, "ans", axis=1, tiled=True)
    prompt_rows = gathered.shape[1]
    plen = prompt_len[0]
    length = ans_len[0]
    columns = jnp.arange(prompt_rows)
    first = lax.axis_index("ans") * piece
    ans_total = alen * group
    pr_total = piece * group
    ans_block = min(512, ans_total)
    token = jnp.arange(ans_total) // group
    own_cols = jnp.arange(alen)
    prompt_pos = first + jnp.arange(pr_total) // group
    dq_a, dk_a, dv_a, dq_p, dk_p, dv_p = ([], [], [], [], [], [])
    kcols = slice(0, HD)
    keys_p = gathered[0, :, kcols]
    vals_p = gathered[1, :, kcols]
    keys_all = jnp.concatenate([keys_p, kv_ans[0, :, kcols]], 0)
    vals_all = jnp.concatenate([vals_p, kv_ans[1, :, kcols]], 0)
    q_rows = q_ans.reshape(ans_total, HD)
    g_rows = dout_ans.reshape(ans_total, HD)
    g_rows = jnp.where((token < length)[:, None], g_rows, jnp.zeros((), jnp.bfloat16))
    prompt_term_k = jnp.zeros((prompt_rows, HD), jnp.float32)
    prompt_term_v = jnp.zeros((prompt_rows, HD), jnp.float32)
    own_k = jnp.zeros((alen, HD), jnp.float32)
    own_v = jnp.zeros((alen, HD), jnp.float32)
    dq_blocks = []
    for start in range(0, ans_total, ans_block):
        rows = q_rows[start : start + ans_block]
        grads_in = g_rows[start : start + ans_block]
        block_tok = token[start : start + ans_block]
        limit = jnp.full((ans_block,), prompt_rows, jnp.int32)
        mask = jnp.concatenate(
            [prompt_mask(columns, limit, plen), own_cols[None, :] <= block_tok[:, None]], 1
        )
        prob_b, dscore, dquery, top, total, delta = block_pass(
            rows, grads_in, keys_all, vals_all, mask, scale
        )
        dq_blocks.append(dquery)
        dkey, dvalue = key_grads(prob_b, dscore, rows, grads_in)
        prompt_term_k = prompt_term_k + dkey[:prompt_rows]
        prompt_term_v = prompt_term_v + dvalue[:prompt_rows]
        own_k = own_k + dkey[prompt_rows:]
        own_v = own_v + dvalue[prompt_rows:]
    dq_a.append(jnp.concatenate(dq_blocks, 0).reshape(alen, group * HD).astype(jnp.bfloat16))
    dk_a.append(own_k)
    dv_a.append(own_v)
    p_rows = q_prompt.reshape(pr_total, HD)
    p_grads = dout_prompt.reshape(pr_total, HD)
    p_grads = jnp.where((prompt_pos < plen)[:, None], p_grads, jnp.zeros((), jnp.bfloat16))
    mask = prompt_mask(columns, prompt_pos, plen)
    prob_b, dscore, dquery, top, total, delta = block_pass(
        p_rows, p_grads, keys_p, vals_p, mask, scale
    )
    dkey, dvalue = key_grads(prob_b, dscore, p_rows, p_grads)
    prompt_term_k = prompt_term_k + dkey
    prompt_term_v = prompt_term_v + dvalue
    dq_p.append(dquery.reshape(piece, group * HD).astype(jnp.bfloat16))
    dk_p.append(prompt_term_k)
    dv_p.append(prompt_term_v)
    term = jnp.stack([dk_p[0], dv_p[0]], axis=1)
    summed = lax.psum_scatter(term, "ans", scatter_dimension=0, tiled=True)
    d_q_ans = dq_a[0]
    d_kv_ans = jnp.stack([dk_a[0], dv_a[0]]).astype(jnp.bfloat16)
    d_q_prompt = dq_p[0]
    d_kv_prompt = jnp.transpose(summed, (1, 0, 2)).astype(jnp.bfloat16)
    return (d_q_ans, d_kv_ans, d_q_prompt, d_kv_prompt)


def solution(mesh):
    in_specs = (
        P(("group", "ans"), "tp"),
        P(None, ("group", "ans"), "tp"),
        P(("group", "ans"), "tp"),
        P(None, ("group", "ans"), "tp"),
        P(("group", "ans"), "tp"),
        P(("group", "ans"), "tp"),
        P(("group", "ans")),
        P("group"),
    )
    out_specs = (
        P(("group", "ans"), "tp"),
        P(None, ("group", "ans"), "tp"),
        P(("group", "ans"), "tp"),
        P(None, ("group", "ans"), "tp"),
    )
    return jax.shard_map(
        per_device, mesh=mesh, in_specs=in_specs, out_specs=out_specs, check_vma=False
    )
```

profile of v0, /device:TPU:24, one launch (start us, length us, event | category | flops | bytes accessed | tf_op | source)
XLA Modules:
  0.0 308.0 jit_solution(4722514067121924989)
XLA Ops:
  8.0 1.0 fusion.49
  9.7 1.1 reshape.78
  13.7 132.6 %all-gather.2.cloned.1.call-done = bf16[2,2048,128]{2,1,0:T(8,128)(2,1)} async-done(((bf16[2,64,128]{2,1,0:T(8,128)(2,1)}), bf16[2,2048,128]{2,1,0:T(8,128)(2,1)}) %all-gather.2.cloned.1.call-update) | async-done | bytes 1048592 | tf_op jit(solution)/shard_map/all_gather | solution.py:51
  146.3 1.3 slice_bitcast_fusion
  147.6 0.8 fusion.51
  149.7 0.8 fusion.52
  151.9 0.7 fusion.26
  153.7 0.7 fusion.29
  154.5 1.2 fusion.9
  155.7 1.2 fusion.8
  158.4 0.7 fusion.54
  159.7 1.6 fusion.53
  162.0 0.8 fusion.15
  162.8 0.7 fusion.17
  163.6 0.8 fusion.23
  165.2 0.8 fusion.18
  166.6 1.5 pad_maximum_fusion
  168.1 2.7 convolution_convert_fusion.1
  170.8 0.8 convolution_convert_fusion.2
  172.3 1.8 convert_element_type.50
  174.0 2.4 convolution_convert_fusion
  177.1 0.8 fusion.38
  178.7 121.0 %reduce-scatter.2.cloned.1.call-done = f32[64,2,128]{2,0,1:T(8,128)} async-done(((f32[2048,2,128]{2,0,1:T(8,128)}), f32[64,2,128]{2,0,1:T(8,128)}) %reduce-scatter.2.cloned.1.call-update) | async-done | bytes 65552 | tf_op jit(solution)/shard_map/reduce_scatter | solution.py:111
  299.7 1.5 convert_bitcast_fusion
  (67 shorter events, 13.0 us)
Async XLA Ops:
  7.2 4.5 %copy-start.13 = (bf16[64,1024]{1,0:T(8,128)(2,1)S(1)}, bf16[64,1024]{1,0:T(8,128)(2,1)}, u32[]{:S(2)}) copy-start(bf16[64,1024]{1,0:T(8,128)(2,1)} %param.10) | copy-start | bytes 393220
  7.2 5.2 %copy-start.9 = (bf16[64,1024]{1,0:T(8,128)(2,1)S(1)}, bf16[64,1024]{1,0:T(8,128)(2,1)}, u32[]{:S(2)}) copy-start(bf16[64,1024]{1,0:T(8,128)(2,1)} %param.13) | copy-start | bytes 393220
  7.2 6.4 %copy-start.14 = (bf16[2,128,128]{2,1,0:T(8,128)(2,1)S(1)}, bf16[2,128,128]{2,1,0:T(8,128)(2,1)}, u32[]{:S(2)}) copy-start(bf16[2,128,128]{2,1,0:T(8,128)(2,1)} %param.9) | copy-start | bytes 196612
  7.2 139.1 %all-gather.2.cloned.1.call-start = ((), (), s32[]{:S(2)}) async-start(), calls=%async_computation.1 | async-start | bytes 1081344 | tf_op jit(solution)/shard_map/all_gather | solution.py:51
  7.9 291.7 %reduce-scatter.2.cloned.1.call-start = ((), (), s32[]{:S(2)}) async-start(), calls=%async_computation.2 | async-start | bytes 2162688 | tf_op jit(solution)/shard_map/reduce_scatter | solution.py:111
  11.6 138.1 %copy-start.6 = (bf16[512,128]{1,0:T(8,128)(2,1)}, bf16[512,128]{1,0:T(8,128)(2,1)S(1)}, u32[]{:S(2)}) copy-start(bf16[512,128]{1,0:T(8,128)(2,1)S(1)} %slice.64) | copy-start | bytes 393220
  147.5 2.2 copy-start.10
  154.5 8.3 %copy-start = (f32[2176,128]{1,0:T(8,128)}, f32[2176,128]{1,0:T(8,128)S(1)}, u32[]{:S(2)}) copy-start(f32[2176,128]{1,0:T(8,128)S(1)} %fusion.29) | copy-start | bytes 3342340
  155.7 1.4 copy-start.2
  157.0 1.4 copy-start.3
  157.0 1.4 copy-start.7
  158.4 1.2 copy-start.5
  158.4 1.2 copy-start.12
  163.6 0.9 copy-start.8
  165.2 1.4 copy-start.1
  168.1 2.7 copy-start.4
  168.1 2.7 copy-start.11
Sparse Core Ops, SparseCore 0:
  10.1 136.1 all-gather.1
  168.2 131.4 reduce-scatter.1
where the time goes:
time: 309 us; the launch traced here: 308 us
  waiting for transfers between devices  254 us (82%)
  matrix products  18.5 us (6%)
  between operations  15.8 us (5%)
  local copies, waits for them, and re-layouts  9.79 us (3%)
  other arithmetic  9.63 us (3%)
    all_gather x1, waiting for transfers between devices, per_device(): gathered = lax.all_gather(kv_prompt, 'ans', axis=1, tiled=True)  133 us
    reduce_scatter x1, waiting for transfers between devices, per_device(): summed = lax.psum_scatter(term, 'ans', scatter_dimension=0, tiled=True)  121 us
  transfers between devices with their start and end apart: 2, of which 2 were waited for; matrix products, arithmetic and copies ran while one was open for 5% of the time, Pallas kernels for 0%

commit v1 on v0

v1 whole, which is shorter than its diff:
```python
import functools
import math

import jax
import jax.numpy as jnp
from jax import lax
from jax.experimental import pallas as pl
from jax.experimental.pallas import tpu as pltpu
from jax.sharding import PartitionSpec as P

MESH = pl.DeviceIdType.MESH
F32, BF16 = jnp.float32, jnp.bfloat16
HD = 128
HEADS = 8
ALEN = 128
PIECE = 64
A_ROWS = HEADS * ALEN
P_ROWS = HEADS * PIECE
ROWS = A_ROWS + P_ROWS
LANES = 256
CHUNKS = ROWS // LANES
SCALE = 1.0 / math.sqrt(HD)
COEF = SCALE * math.log2(math.e)
NEG = -1e30
NT = (((1,), (1,)), ((), ()))


def kernel(nz, ans_len, prompt_len, q_a, kv_a, q_p, kv_p, g_a, g_p,
           dq_a, dkv_a, dq_p, dkv_p,
           kv, kt, q, g, e, dp, ds, pbuf, mrun, tot, mgrp, rgrp, delta,
           terms, dq, own_out, prm_out, rs_in, rs_out, x_in, x_out,
           ld_sem, st_sem, ag_send, ag_recv, gx_send, gx_recv,
           rs_send, rs_recv, rx_send, rx_recv):
    half = nz // 2
    me = lax.axis_index("ans")
    par = me // nz
    z = me % nz
    right = par * nz + (z + 1) % nz
    left = par * nz + (z + nz - 1) % nz
    cross = (1 - par) * nz + z
    alen = ans_len[0]
    plen = prompt_len[0]
    n_keys = 256 * half + 128

    def towards(d):
        return {"ans": right if d == 0 else left}

    for h in range(HEADS):
        cols = pl.ds(h * HD, HD)
        pltpu.make_async_copy(q_a.at[:, cols], q.at[pl.ds(h * ALEN, ALEN)], ld_sem.at[0]).start()
        pltpu.make_async_copy(q_p.at[:, cols], q.at[pl.ds(A_ROWS + h * PIECE, PIECE)], ld_sem.at[0]).start()
        pltpu.make_async_copy(g_a.at[:, cols], g.at[pl.ds(h * ALEN, ALEN)], ld_sem.at[1]).start()
        pltpu.make_async_copy(g_p.at[:, cols], g.at[pl.ds(A_ROWS + h * PIECE, PIECE)], ld_sem.at[1]).start()
    own_row = pl.multiple_of(par * PIECE, PIECE)
    cross_row = pl.multiple_of((1 - par) * PIECE, PIECE)
    own_load = pltpu.make_async_copy(kv_p, kv.at[:, pl.ds(own_row, PIECE)], ld_sem.at[2])
    own_load.start()
    ans_load = pltpu.make_async_copy(kv_a, kv.at[:, pl.ds(128, ALEN)], ld_sem.at[3])
    ans_load.start()

    barrier = pltpu.get_barrier_semaphore()
    for peer in (right, left, cross):
        pl.semaphore_signal(barrier, inc=1, device_id={"ans": peer}, device_id_type=MESH)
    pl.semaphore_wait(barrier, 3)

    def block_row(s, d, r):
        return pl.multiple_of(s * 256 + d * 128 + r * PIECE, PIECE)

    def hop(s, d, c, r, src=None):
        first = isinstance(s, int) and s == 1
        last = isinstance(s, int) and s == half
        if src is None:
            row = pl.multiple_of(r * PIECE, PIECE) if first else block_row(s - 1, d, r)
            src = kv.at[c, pl.ds(row, PIECE)]
        row = 256 * half + r * PIECE if last else block_row(s, d, r)
        return pltpu.make_async_remote_copy(
            src_ref=src, dst_ref=kv.at[c, pl.ds(row, PIECE)],
            send_sem=ag_send.at[d, c, r], recv_sem=ag_recv.at[s - 1, d, c, r],
            device_id=towards(d), device_id_type=MESH)

    def exchange(c):
        return pltpu.make_async_remote_copy(
            src_ref=kv_p.at[c], dst_ref=kv.at[c, pl.ds(own_row, PIECE)],
            send_sem=gx_send.at[c], recv_sem=gx_recv.at[c],
            device_id={"ans": cross}, device_id_type=MESH)

    def arrival(c):
        return pltpu.make_async_remote_copy(
            src_ref=kv_p.at[c], dst_ref=kv.at[c, pl.ds(cross_row, PIECE)],
            send_sem=gx_send.at[c], recv_sem=gx_recv.at[c],
            device_id={"ans": cross}, device_id_type=MESH)

    for c in range(2):
        exchange(c).start()
        for d in range(2):
            hop(1, d, c, par, kv_p.at[c]).start()
    for c in range(2):
        arrival(c).wait_recv()
        for d in range(2):
            hop(1, d, c, 1 - par).start()

    pltpu.make_async_copy(q, q, ld_sem.at[0]).wait()
    pltpu.make_async_copy(g, g, ld_sem.at[1]).wait()
    own_load.wait()
    ans_load.wait()
    tok = lax.broadcasted_iota(jnp.int32, (A_ROWS, HD), 0) & (ALEN - 1)
    g[0:A_ROWS] = jnp.where(tok < alen, g[0:A_ROWS], jnp.zeros((), BF16))
    tok = me * PIECE + (lax.broadcasted_iota(jnp.int32, (P_ROWS, HD), 0) & (PIECE - 1))
    g[A_ROWS:ROWS] = jnp.where(tok < plen, g[A_ROWS:ROWS], jnp.zeros((), BF16))

    def limits(j):
        lane = lax.broadcasted_iota(jnp.int32, (1, LANES), 1)
        if j * LANES < A_ROWS:
            return jnp.zeros((1, LANES), jnp.int32) + (plen - 1), lane & (ALEN - 1)
        pos = me * PIECE + (lane & (PIECE - 1))
        return jnp.minimum(pos, plen - 1), jnp.full((1, LANES), -1, jnp.int32)

    def score_group(s, off, bases, own):
        n = PIECE * len(bases) + (ALEN if own else 0)
        rows = pl.ds(off, n)
        keys = kv[0, rows, :]
        values = kv[1, rows, :]
        for j in range(CHUNKS):
            lanes = slice(j * LANES, (j + 1) * LANES)
            lim, lim_own = limits(j)
            raw = lax.dot_general(keys, q[lanes, :], NT, preferred_element_type=F32)
            parts = []
            for b, base in enumerate(bases):
                pos = base + lax.broadcasted_iota(jnp.int32, (PIECE, LANES), 0)
                parts.append(jnp.where(pos <= lim, raw[b * PIECE:(b + 1) * PIECE], NEG))
            if own:
                pos = lax.broadcasted_iota(jnp.int32, (ALEN, LANES), 0)
                parts.append(jnp.where(pos <= lim_own, raw[n - ALEN:n], NEG))
            raw = jnp.concatenate(parts, 0).reshape(n // 8, 8, LANES)
            high = jnp.max(raw, axis=0)
            if own:
                new = high
            else:
                old = mrun[:, lanes]
                new = jnp.maximum(old, high)
            ex = jnp.exp2((raw - new[None]) * COEF)
            part = jnp.sum(ex, axis=0)
            if own:
                tot[:, lanes] = part
            else:
                tot[:, lanes] = tot[:, lanes] * jnp.exp2((old - new) * COEF) + part
            mrun[:, lanes] = new
            mgrp[s, :, lanes] = new
            e[rows, lanes] = ex.reshape(n, LANES)
            dp[rows, lanes] = lax.dot_general(values, g[lanes, :], NT, preferred_element_type=F32)

    def base_of(s, d, r):
        there = (z + nz - s) % nz if d == 0 else (z + s) % nz
        return (r * nz + there) * PIECE

    score_group(0, 0, [base_of(0, 0, 0), base_of(0, 0, 1)], True)

    def middle(s, carry):
        for r in (par, 1 - par):
            for c in range(2):
                for d in range(2):
                    hop(s, d, c, r).wait()
                    hop(s + 1, d, c, r).start()
        score_group(s, pl.multiple_of(s * 256, 256),
                    [base_of(s, d, r) for d in range(2) for r in range(2)], False)
        return carry

    for r in (par, 1 - par):
        for c in range(2):
            for d in range(2):
                hop(1, d, c, r).wait()
                hop(2, d, c, r).start()
    score_group(1, 256, [base_of(1, d, r) for d in range(2) for r in range(2)], False)
    lax.fori_loop(2, half - 1, middle, 0)
    s = half - 1
    for r in range(2):
        for c in range(2):
            for d in range(2):
                hop(s, d, c, r).wait()
                if r == d:
                    hop(half, d, c, r).start()
    score_group(s, s * 256, [base_of(s, d, r) for d in range(2) for r in range(2)], False)
    for c in range(2):
        for d in range(2):
            hop(half, d, c, d).wait()
    for c in range(2):
        exchange(c).wait_send()
    score_group(half, half * 256, [base_of(half, d, d) for d in range(2)], False)

    m8 = mrun[...]
    top = jnp.max(m8, axis=0, keepdims=True)
    total = jnp.sum(tot[...] * jnp.exp2((m8 - top) * COEF), axis=0, keepdims=True)
    inv = 1.0 / total
    for s in range(half + 1):
        rgrp[s] = jnp.exp2((mgrp[s] - top) * COEF) * inv
    delta[...] = jnp.zeros_like(delta)

    def rows_of(s):
        return pl.multiple_of(s * 256, 256) if not isinstance(s, int) else s * 256

    def value_terms(s, n=256):
        rows = pl.ds(rows_of(s), n)
        for j in range(CHUNKS):
            lanes = slice(j * LANES, (j + 1) * LANES)
            p = e[rows, lanes].reshape(n // 8, 8, LANES) * rgrp[s, :, lanes][None]
            pb = p.reshape(n, LANES).astype(BF16)
            pbuf[0:n, lanes] = pb
            prod = pb.astype(F32) * dp[rows, lanes]
            delta[:, lanes] += jnp.sum(prod.reshape(n // 8, 8, LANES), axis=0)
        terms[1, rows, :] = jnp.dot(pbuf[0:n], g[...], preferred_element_type=F32)

    def key_terms(s, n=256):
        rows = pl.ds(rows_of(s), n)
        for j in range(CHUNKS):
            lanes = slice(j * LANES, (j + 1) * LANES)
            p = e[rows, lanes].reshape(n // 8, 8, LANES) * (rgrp[s, :, lanes] * SCALE)[None]
            diff = dp[rows, lanes].reshape(n // 8, 8, LANES) - delta[:, lanes][None]
            ds[rows, lanes] = (p * diff).reshape(n, LANES).astype(BF16)
        terms[0, rows, :] = jnp.dot(ds[rows, :], q[...], preferred_element_type=F32)

    def query_terms(j):
        lanes = slice(j * LANES, (j + 1) * LANES)
        flipped = jnp.dot(kt[...], ds[:, lanes], preferred_element_type=F32)
        dq[lanes, :] = flipped.T.astype(BF16)

    def run(fn, first, last):
        if first >= last:
            lax.fori_loop(0, first - last + 1, lambda i, carry: (fn(first - i), carry)[1], 0)

    def partial_sum(far, d, c, r):
        return pltpu.make_async_remote_copy(
            src_ref=rs_out.at[far - 1, d, c, r], dst_ref=rs_in.at[far - 1, d, c, r],
            send_sem=rs_send.at[d, c, r], recv_sem=rs_recv.at[far - 1, d, c, r],
            device_id=towards(d), device_id_type=MESH)

    def ring(c, far):
        for r in range(2):
            for d in range(2):
                if far == half:
                    if r != d:
                        continue
                    row = half * 256 + r * PIECE
                else:
                    row = far * 256 + (1 - d) * 128 + r * PIECE
                term = terms[c, row:row + PIECE, :]
                if far < half - 1 or (far == half - 1 and r == d):
                    partial_sum(far + 1, d, c, r).wait()
                    term = term + rs_in[far, d, c, r].astype(F32)
                rs_out[far - 1, d, c, r] = term.astype(BF16)
                partial_sum(far, d, c, r).start()

    def swap(c):
        return pltpu.make_async_remote_copy(
            src_ref=x_out.at[c], dst_ref=x_in.at[c],
            send_sem=rx_send.at[c], recv_sem=rx_recv.at[c],
            device_id={"ans": cross}, device_id_type=MESH)

    def gathered_sum(c, row, r):
        acc = terms[c, pl.ds(row, PIECE), :]
        for d in range(2):
            partial_sum(1, d, c, r).wait()
            acc = acc + rs_in[0, d, c, r].astype(F32)
        return acc

    def finish(c):
        x_out[c] = gathered_sum(c, cross_row, 1 - par).astype(BF16)
        swap(c).start()
        terms[c, pl.ds(own_row, PIECE), :] = gathered_sum(c, own_row, par)

    def settle(c):
        swap(c).wait()
        prm_out[c] = (terms[c, pl.ds(own_row, PIECE), :] + x_in[c].astype(F32)).astype(BF16)

    K, V = 0, 1
    value_terms(half, 128)
    ring(V, half)
    run(value_terms, half - 1, half // 2)
    ring(V, half - 1)
    run(value_terms, half // 2 - 1, 0)
    delta[...] = jnp.broadcast_to(jnp.sum(delta[...], axis=0, keepdims=True), delta.shape)
    key_terms(half, 128)
    ring(K, half)
    vnext = half - 2
    knext = half - 1
    ring(V, vnext)
    group = half - 1
    while group >= 0:
        low = max(group - 1, 0)
        run(key_terms, group, low)
        group = low - 1
        ring(K, knext)
        knext -= 1
        vnext -= 1
        if vnext >= 1:
            ring(V, vnext)
        elif vnext == 0:
            finish(V)
    own_out[...] = terms[:, 128:256, :].astype(BF16)
    for s in range(n_keys // 128):
        kt[:, s * 128:(s + 1) * 128] = kv[0, s * 128:(s + 1) * 128, :].T
    for j in range(CHUNKS):
        query_terms(j)
        if j % 2 == 1:
            if knext >= 1:
                ring(K, knext)
                knext -= 1
            vnext -= 1
            if vnext >= 1:
                ring(V, vnext)
            elif vnext == 0:
                finish(V)
    stores = [pltpu.make_async_copy(own_out, dkv_a, st_sem.at[0])]
    stores[0].start()
    for h in range(HEADS):
        cols = pl.ds(h * HD, HD)
        pltpu.make_async_copy(dq.at[pl.ds(h * ALEN, ALEN)], dq_a.at[:, cols], st_sem.at[1]).start()
        pltpu.make_async_copy(dq.at[pl.ds(A_ROWS + h * PIECE, PIECE)], dq_p.at[:, cols], st_sem.at[1]).start()
    while knext >= 1:
        ring(K, knext)
        knext -= 1
    finish(K)
    settle(V)
    settle(K)
    out = pltpu.make_async_copy(prm_out, dkv_p, st_sem.at[2])
    out.start()
    stores[0].wait()
    pltpu.make_async_copy(dq, dq, st_sem.at[1]).wait()
    out.wait()


def per_device(nz, q_ans, kv_ans, q_prompt, kv_prompt, dout_ans, dout_prompt, ans_len, prompt_len):
    half = nz // 2
    n_keys = 256 * half + 128
    any_spec = pl.BlockSpec(memory_space=pl.ANY)
    smem = pl.BlockSpec(memory_space=pltpu.SMEM)
    dma, vm = pltpu.SemaphoreType.DMA, pltpu.VMEM
    blocks = (half, 2, 2, 2)
    return pl.pallas_call(
        functools.partial(kernel, nz),
        out_shape=(
            jax.ShapeDtypeStruct(q_ans.shape, BF16),
            jax.ShapeDtypeStruct(kv_ans.shape, BF16),
            jax.ShapeDtypeStruct(q_prompt.shape, BF16),
            jax.ShapeDtypeStruct(kv_prompt.shape, BF16),
        ),
        in_specs=[smem, smem] + [any_spec] * 6,
        out_specs=(any_spec,) * 4,
        scratch_shapes=[
            vm((2, n_keys, HD), BF16),
            vm((HD, n_keys), BF16),
            vm((ROWS, HD), BF16),
            vm((ROWS, HD), BF16),
            vm((n_keys, ROWS), F32),
            vm((n_keys, ROWS), F32),
            vm((n_keys, ROWS), BF16),
            vm((256, ROWS), BF16),
            vm((8, ROWS), F32),
            vm((8, ROWS), F32),
            vm((half + 1, 8, ROWS), F32),
            vm((half + 1, 8, ROWS), F32),
            vm((8, ROWS), F32),
            vm((2, n_keys, HD), F32),
            vm((ROWS, HD), BF16),
            vm((2, ALEN, HD), BF16),
            vm((2, PIECE, HD), BF16),
            vm(blocks + (PIECE, HD), BF16),
            vm(blocks + (PIECE, HD), BF16),
            vm((2, PIECE, HD), BF16),
            vm((2, PIECE, HD), BF16),
            dma((4,)), dma((3,)),
            dma((2, 2, 2)), dma(blocks), dma((2,)), dma((2,)),
            dma((2, 2, 2)), dma(blocks), dma((2,)), dma((2,)),
        ],
        compiler_params=pltpu.CompilerParams(
            collective_id=0, has_side_effects=True, vmem_limit_bytes=58 * 1024 * 1024),
    )(ans_len, prompt_len, q_ans, kv_ans, q_prompt, kv_prompt, dout_ans, dout_prompt)


def solution(mesh):
    in_specs = (
        P(("group", "ans"), "tp"),
        P(None, ("group", "ans"), "tp"),
        P(("group", "ans"), "tp"),
        P(None, ("group", "ans"), "tp"),
        P(("group", "ans"), "tp"),
        P(("group", "ans"), "tp"),
        P(("group", "ans")),
        P("group"),
    )
    out_specs = (
        P(("group", "ans"), "tp"),
        P(None, ("group", "ans"), "tp"),
        P(("group", "ans"), "tp"),
        P(None, ("group", "ans"), "tp"),
    )
    return jax.shard_map(
        functools.partial(per_device, mesh.shape["ans"] // 2), mesh=mesh,
        in_specs=in_specs, out_specs=out_specs, check_vma=False)
```

time: 309 us -> 80.5 us (0.26)
  waiting for transfers between devices: 254 us -> 0 us
  Pallas kernels: 0 us -> 74.1 us
  matrix products: 18.5 us -> 0 us
  between operations: 15.8 us -> 1.94 us
  other arithmetic: 9.63 us -> 0 us
  local copies, waits for them, and re-layouts: 9.79 us -> 4 us
    all_gather x1 -> x0, waiting for transfers between devices: 133 us -> none  [per_device(): gathered = lax.all_gather(kv_prompt, 'ans', axis=1, tiled=True)]
    reduce_scatter x1 -> x0, waiting for transfers between devices: 121 us -> none  [per_device(): summed = lax.psum_scatter(term, 'ans', scatter_dimension=0, tiled=True)]
    pallas_call x0 -> x1, Pallas kernels: none -> 74.1 us  [per_device(): pl.pallas_call(functools.partial(kernel, nz), out_shape=(jax.ShapeDtypeSt...]
    dot_general x18 -> x0, matrix products: 18.5 us -> none  [the longest x3 5.82 us: block_pass(): dquery = jnp.dot(dscore, keys, preferred_element_type=jnp.float32)]
  transfers between devices with their start and end apart: 2 -> 0, of which waited for: 2 -> 0; matrix products, arithmetic and copies ran while one was open for 5% -> 0% of each run, Pallas kernels for 0% -> 0%
where the time goes in v1:
time: 80.5 us; the launch traced here: 80.1 us
  Pallas kernels  74.1 us (92%)
  local copies, waits for them, and re-layouts  4 us (5%)
  between operations  1.94 us (2%)
    pallas_call x1, Pallas kernels, per_device(): pl.pallas_call(functools.partial(kernel, nz), out_shape=(jax.ShapeDtypeSt...  74.1 us
    unnamed x10, local copies, waits for them, and re-layouts  4 us

profile of v1, /device:TPU:24, one launch (start us, length us, event | category | flops | bytes accessed | tf_op | source)
XLA Modules:
  0.0 80.1 jit_solution(3587018863691327357)
XLA Ops:
  1.9 74.1 %shard_map.111 = (bf16[128,1024]{1,0:T(8,128)(2,1)}, bf16[2,128,128]{2,1,0:T(8,128)(2,1)}, bf16[64,1024]{1,0:T(8,128)(2,1)}, bf16[2,64,128]{2,1,0:T(8,128)(2,1)}) custom-call(s32[1]{0:T(128)S(6)} %copy.16.ans_len, s32[1]{0:T(128)S(6)} %copy.17.prompt_len, bf16[128,1024]{1,0:T(8,128)(2,1)} %q_a.1, bf16[2,128,128]{2,1,0:T(8,128)(2,1)} %kv_a.1, ...), custom_call_target="tpu_custom_call" | custom-call | tf_op jit(solution)/shard_map/pallas_call | solution.py:338
  76.0 0.0 copy-start.1
  76.1 1.7 %copy.18 = bf16[128,1024]{1,0:T(8,128)(2,1)} copy(bf16[128,1024]{1,0:T(8,128)(2,1)} %get-tuple-element.8) | data formatting | bytes 524288
  77.8 0.0 copy-done.1
  77.8 0.0 copy-start
  77.8 0.6 copy.19
  78.4 0.3 copy-done
  78.7 0.0 copy-start.2
  78.7 0.7 copy.20
  79.3 0.1 copy-done.2
  79.5 0.6 copy.21
Async XLA Ops:
  76.0 1.7 %copy-start.1 = (bf16[2,128,128]{2,1,0:T(8,128)(2,1)S(1)}, bf16[2,128,128]{2,1,0:T(8,128)(2,1)}, u32[]{:S(2)}) copy-start(bf16[2,128,128]{2,1,0:T(8,128)(2,1)} %get-tuple-element.9) | copy-start | bytes 196612
  77.8 0.9 %copy-start = (bf16[64,1024]{1,0:T(8,128)(2,1)S(1)}, bf16[64,1024]{1,0:T(8,128)(2,1)}, u32[]{:S(2)}) copy-start(bf16[64,1024]{1,0:T(8,128)(2,1)} %get-tuple-element.10) | copy-start | bytes 393220
  78.7 0.8 copy-start.2

commit v2 on v1

--- a/solution.py
+++ b/solution.py
@@ -25,38 +25,21 @@
 NT = (((1,), (1,)), ((), ()))
 
 
-def kernel(nz, ans_len, prompt_len, q_a, kv_a, q_p, kv_p, g_a, g_p,
-           dq_a, dkv_a, dq_p, dkv_p,
-           kv, kt, q, g, e, dp, ds, pbuf, mrun, tot, mgrp, rgrp, delta,
-           terms, dq, own_out, prm_out, rs_in, rs_out, x_in, x_out,
-           ld_sem, st_sem, ag_send, ag_recv, gx_send, gx_recv,
-           rs_send, rs_recv, rx_send, rx_recv):
+def gather(nz, kv_p, kv_out, kv, ld_sem, ag_send, ag_recv, gx_send, gx_recv):
     half = nz // 2
     me = lax.axis_index("ans")
     par = me // nz
     z = me % nz
+    own_load = pltpu.make_async_copy(kv_p, kv.at[:, pl.ds(pl.multiple_of(par * PIECE, PIECE), PIECE)], ld_sem.at[0])
+    own_load.start()
     right = par * nz + (z + 1) % nz
     left = par * nz + (z + nz - 1) % nz
     cross = (1 - par) * nz + z
-    alen = ans_len[0]
-    plen = prompt_len[0]
-    n_keys = 256 * half + 128
+    own_row = pl.multiple_of(par * PIECE, PIECE)
+    cross_row = pl.multiple_of((1 - par) * PIECE, PIECE)
 
     def towards(d):
         return {"ans": right if d == 0 else left}
-
-    for h in range(HEADS):
-        cols = pl.ds(h * HD, HD)
-        pltpu.make_async_copy(q_a.at[:, cols], q.at[pl.ds(h * ALEN, ALEN)], ld_sem.at[0]).start()
-        pltpu.make_async_copy(q_p.at[:, cols], q.at[pl.ds(A_ROWS + h * PIECE, PIECE)], ld_sem.at[0]).start()
-        pltpu.make_async_copy(g_a.at[:, cols], g.at[pl.ds(h * ALEN, ALEN)], ld_sem.at[1]).start()
-        pltpu.make_async_copy(g_p.at[:, cols], g.at[pl.ds(A_ROWS + h * PIECE, PIECE)], ld_sem.at[1]).start()
-    own_row = pl.multiple_of(par * PIECE, PIECE)
-    cross_row = pl.multiple_of((1 - par) * PIECE, PIECE)
-    own_load = pltpu.make_async_copy(kv_p, kv.at[:, pl.ds(own_row, PIECE)], ld_sem.at[2])
-    own_load.start()
-    ans_load = pltpu.make_async_copy(kv_a, kv.at[:, pl.ds(128, ALEN)], ld_sem.at[3])
-    ans_load.start()
 
     barrier = pltpu.get_barrier_semaphore()
     for peer in (right, left, cross):
@@ -99,10 +82,65 @@
         for d in range(2):
             hop(1, d, c, 1 - par).start()
 
+    own_load.wait()
+
+    def middle(s, carry):
+        for r in (par, 1 - par):
+            for c in range(2):
+                for d in range(2):
+                    hop(s, d, c, r).wait()
+                    hop(s + 1, d, c, r).start()
+        return carry
+
+    for r in (par, 1 - par):
+        for c in range(2):
+            for d in range(2):
+                hop(1, d, c, r).wait()
+                hop(2, d, c, r).start()
+    lax.fori_loop(2, half - 1, middle, 0)
+    s = half - 1
+    for r in range(2):
+        for c in range(2):
+            for d in range(2):
+                hop(s, d, c, r).wait()
+                if r == d:
+                    hop(half, d, c, r).start()
+    for c in range(2):
+        for d in range(2):
+            hop(half, d, c, d).wait()
+    for c in range(2):
+        exchange(c).wait_send()
+    out = pltpu.make_async_copy(kv, kv_out, ld_sem.at[0])
+    out.start()
+    out.wait()
+
+
+def attend(nz, ans_len, prompt_len, q_a, kv_a, q_p, kv_all, g_a, g_p,
+           dq_a, dkv_a, dq_p, terms_out,
+           kv, kt, q, g, e, dp, ds, pbuf, mrun, tot, mgrp, rgrp, delta,
+           terms, dq, own_out, ld_sem, st_sem):
+    half = nz // 2
+    me = lax.axis_index("ans")
+    par = me // nz
+    z = me % nz
+    alen = ans_len[0]
+    plen = prompt_len[0]
+    n_keys = 256 * half + 128
+    for h in range(HEADS):
+        cols = pl.ds(h * HD, HD)
+        pltpu.make_async_copy(q_a.at[:, cols], q.at[pl.ds(h * ALEN, ALEN)], ld_sem.at[0]).start()
+        pltpu.make_async_copy(q_p.at[:, cols], q.at[pl.ds(A_ROWS + h * PIECE, PIECE)], ld_sem.at[0]).start()
+        pltpu.make_async_copy(g_a.at[:, cols], g.at[pl.ds(h * ALEN, ALEN)], ld_sem.at[1]).start()
+        pltpu.make_async_copy(g_p.at[:, cols], g.at[pl.ds(A_ROWS + h * PIECE, PIECE)], ld_sem.at[1]).start()
+    loads = [pltpu.make_async_copy(kv_all.at[:, pl.ds(0, 128)], kv.at[:, pl.ds(0, 128)], ld_sem.at[2]),
+             pltpu.make_async_copy(kv_all.at[:, pl.ds(256, n_keys - 256)], kv.at[:, pl.ds(256, n_keys - 256)], ld_sem.at[3]),
+             pltpu.make_async_copy(kv_a, kv.at[:, pl.ds(128, ALEN)], ld_sem.at[4])]
+    for load in loads:
+        load.start()
+    for load in loads:
+        load.wait()
     pltpu.make_async_copy(q, q, ld_sem.at[0]).wait()
     pltpu.make_async_copy(g, g, ld_sem.at[1]).wait()
-    own_load.wait()
-    ans_load.wait()
     tok = lax.broadcasted_iota(jnp.int32, (A_ROWS, HD), 0) & (ALEN - 1)
     g[0:A_ROWS] = jnp.where(tok < alen, g[0:A_ROWS], jnp.zeros((), BF16))
     tok = me * PIECE + (lax.broadcasted_iota(jnp.int32, (P_ROWS, HD), 0) & (PIECE - 1))
@@ -153,38 +191,16 @@
         there = (z + nz - s) % nz if d == 0 else (z + s) % nz
         return (r * nz + there) * PIECE
 
+    def four(s):
+        return [base_of(s, d, r) for d in range(2) for r in range(2)]
+
     score_group(0, 0, [base_of(0, 0, 0), base_of(0, 0, 1)], True)
 
     def middle(s, carry):
-        for r in (par, 1 - par):
-            for c in range(2):
-                for d in range(2):
-                    hop(s, d, c, r).wait()
-                    hop(s + 1, d, c, r).start()
-        score_group(s, pl.multiple_of(s * 256, 256),
-                    [base_of(s, d, r) for d in range(2) for r in range(2)], False)
+        score_group(s, pl.multiple_of(s * 256, 256), four(s), False)
         return carry
 
-    for r in (par, 1 - par):
-        for c in range(2):
-            for d in range(2):
-                hop(1, d, c, r).wait()
-                hop(2, d, c, r).start()
-    score_group(1, 256, [base_of(1, d, r) for d in range(2) for r in range(2)], False)
-    lax.fori_loop(2, half - 1, middle, 0)
-    s = half - 1
-    for r in range(2):
-        for c in range(2):
-            for d in range(2):
-                hop(s, d, c, r).wait()
-                if r == d:
-                    hop(half, d, c, r).start()
-    score_group(s, s * 256, [base_of(s, d, r) for d in range(2) for r in range(2)], False)
-    for c in range(2):
-        for d in range(2):
-            hop(half, d, c, d).wait()
-    for c in range(2):
-        exchange(c).wait_send()
+    lax.fori_loop(1, half, middle, 0)
     score_group(half, half * 256, [base_of(half, d, d) for d in range(2)], False)
 
     m8 = mrun[...]
@@ -223,9 +239,50 @@
         flipped = jnp.dot(kt[...], ds[:, lanes], preferred_element_type=F32)
         dq[lanes, :] = flipped.T.astype(BF16)
 
-    def run(fn, first, last):
-        if first >= last:
-            lax.fori_loop(0, first - last + 1, lambda i, carry: (fn(first - i), carry)[1], 0)
+    value_terms(half, 128)
+    lax.fori_loop(0, half, lambda s, carry: (value_terms(s), carry)[1], 0)
+    delta[...] = jnp.broadcast_to(jnp.sum(delta[...], axis=0, keepdims=True), delta.shape)
+    key_terms(half, 128)
+    lax.fori_loop(0, half, lambda s, carry: (key_terms(s), carry)[1], 0)
+    sums = pltpu.make_async_copy(terms, terms_out, st_sem.at[2])
+    sums.start()
+    own_out[...] = terms[:, 128:256, :].astype(BF16)
+    own = pltpu.make_async_copy(own_out, dkv_a, st_sem.at[0])
+    own.start()
+    for s in range(n_keys // 128):
+        kt[:, s * 128:(s + 1) * 128] = kv[0, s * 128:(s + 1) * 128, :].T
+    for j in range(CHUNKS):
+        query_terms(j)
+    for h in range(HEADS):
+        cols = pl.ds(h * HD, HD)
+        pltpu.make_async_copy(dq.at[pl.ds(h * ALEN, ALEN)], dq_a.at[:, cols], st_sem.at[1]).start()
+        pltpu.make_async_copy(dq.at[pl.ds(A_ROWS + h * PIECE, PIECE)], dq_p.at[:, cols], st_sem.at[1]).start()
+    sums.wait()
+    own.wait()
+    pltpu.make_async_copy(dq, dq, st_sem.at[1]).wait()
+
+
+def scatter(nz, terms_in, dkv_p, terms, prm_out, rs_in, rs_out, x_in, x_out,
+            ld_sem, rs_send, rs_recv, rx_send, rx_recv):
+    half = nz // 2
+    me = lax.axis_index("ans")
+    par = me // nz
+    z = me % nz
+    load = pltpu.make_async_copy(terms_in, terms, ld_sem.at[0])
+    load.start()
+    right = par * nz + (z + 1) % nz
+    left = par * nz + (z + nz - 1) % nz
+    cross = (1 - par) * nz + z
+    own_row = pl.multiple_of(par * PIECE, PIECE)
+    cross_row = pl.multiple_of((1 - par) * PIECE, PIECE)
+
+    def towards(d):
+        return {"ans": right if d == 0 else left}
+
+    barrier = pltpu.get_barrier_semaphore()
+    for peer in (right, left, cross):
+        pl.semaphore_signal(barrier, inc=1, device_id={"ans": peer}, device_id_type=MESH)
+    pl.semaphore_wait(barrier, 3)
 
     def partial_sum(far, d, c, r):
         return pltpu.make_async_remote_copy(
@@ -271,60 +328,16 @@
         swap(c).wait()
         prm_out[c] = (terms[c, pl.ds(own_row, PIECE), :] + x_in[c].astype(F32)).astype(BF16)
 
-    K, V = 0, 1
-    value_terms(half, 128)
-    ring(V, half)
-    run(value_terms, half - 1, half // 2)
-    ring(V, half - 1)
-    run(value_terms, half // 2 - 1, 0)
-    delta[...] = jnp.broadcast_to(jnp.sum(delta[...], axis=0, keepdims=True), delta.shape)
-    key_terms(half, 128)
-    ring(K, half)
-    vnext = half - 2
-    knext = half - 1
-    ring(V, vnext)
-    group = half - 1
-    while group >= 0:
-        low = max(group - 1, 0)
-        run(key_terms, group, low)
-        group = low - 1
-        ring(K, knext)
-        knext -= 1
-        vnext -= 1
-        if vnext >= 1:
-            ring(V, vnext)
-        elif vnext == 0:
-            finish(V)
-    own_out[...] = terms[:, 128:256, :].astype(BF16)
-    for s in range(n_keys // 128):
-        kt[:, s * 128:(s + 1) * 128] = kv[0, s * 128:(s + 1) * 128, :].T
-    for j in range(CHUNKS):
-        query_terms(j)
-        if j % 2 == 1:
-            if knext >= 1:
-                ring(K, knext)
-                knext -= 1
-            vnext -= 1
-            if vnext >= 1:
-                ring(V, vnext)
-            elif vnext == 0:
-                finish(V)
-    stores = [pltpu.make_async_copy(own_out, dkv_a, st_sem.at[0])]
-    stores[0].start()
-    for h in range(HEADS):
-        cols = pl.ds(h * HD, HD)
-        pltpu.make_async_copy(dq.at[pl.ds(h * ALEN, ALEN)], dq_a.at[:, cols], st_sem.at[1]).start()
-        pltpu.make_async_copy(dq.at[pl.ds(A_ROWS + h * PIECE, PIECE)], dq_p.at[:, cols], st_sem.at[1]).start()
-    while knext >= 1:
-        ring(K, knext)
-        knext -= 1
-    finish(K)
-    settle(V)
-    settle(K)
-    out = pltpu.make_async_copy(prm_out, dkv_p, st_sem.at[2])
+    load.wait()
+    for far in range(half, 0, -1):
+        ring(1, far)
+        ring(0, far)
+    finish(1)
+    finish(0)
+    settle(1)
+    settle(0)
+    out = pltpu.make_async_copy(prm_out, dkv_p, ld_sem.at[0])
     out.start()
-    stores[0].wait()
-    pltpu.make_async_copy(dq, dq, st_sem.at[1]).wait()
     out.wait()
 
 
@@ -335,13 +348,25 @@
     smem = pl.BlockSpec(memory_space=pltpu.SMEM)
     dma, vm = pltpu.SemaphoreType.DMA, pltpu.VMEM
     blocks = (half, 2, 2, 2)
-    return pl.pallas_call(
-        functools.partial(kernel, nz),
+    gathered = pl.pallas_call(
+        functools.partial(gather, nz),
+        out_shape=jax.ShapeDtypeStruct((2, n_keys, HD), BF16),
+        in_specs=[any_spec],
+        out_specs=any_spec,
+        scratch_shapes=[
+            vm((2, n_keys, HD), BF16), dma((1,)),
+            dma((2, 2, 2)), dma(blocks), dma((2,)), dma((2,)),
+        ],
+        compiler_params=pltpu.CompilerParams(
+            collective_id=0, has_side_effects=True, vmem_limit_bytes=58 * 1024 * 1024),
+    )(kv_prompt)
+    d_q_ans, d_kv_ans, d_q_prompt, terms = pl.pallas_call(
+        functools.partial(attend, nz),
         out_shape=(
             jax.ShapeDtypeStruct(q_ans.shape, BF16),
             jax.ShapeDtypeStruct(kv_ans.shape, BF16),
             jax.ShapeDtypeStruct(q_prompt.shape, BF16),
-            jax.ShapeDtypeStruct(kv_prompt.shape, BF16),
+            jax.ShapeDtypeStruct((2, n_keys, HD), F32),
         ),
         in_specs=[smem, smem] + [any_spec] * 6,
         out_specs=(any_spec,) * 4,
@@ -362,18 +387,29 @@
             vm((2, n_keys, HD), F32),
             vm((ROWS, HD), BF16),
             vm((2, ALEN, HD), BF16),
+            dma((5,)), dma((3,)),
+        ],
+        compiler_params=pltpu.CompilerParams(vmem_limit_bytes=58 * 1024 * 1024),
+    )(ans_len, prompt_len, q_ans, kv_ans, q_prompt, gathered, dout_ans, dout_prompt)
+    d_kv_prompt = pl.pallas_call(
+        functools.partial(scatter, nz),
+        out_shape=jax.ShapeDtypeStruct(kv_prompt.shape, BF16),
+        in_specs=[any_spec],
+        out_specs=any_spec,
+        scratch_shapes=[
+            vm((2, n_keys, HD), F32),
             vm((2, PIECE, HD), BF16),
             vm(blocks + (PIECE, HD), BF16),
             vm(blocks + (PIECE, HD), BF16),
             vm((2, PIECE, HD), BF16),
             vm((2, PIECE, HD), BF16),
-            dma((4,)), dma((3,)),
-            dma((2, 2, 2)), dma(blocks), dma((2,)), dma((2,)),
+            dma((1,)),
             dma((2, 2, 2)), dma(blocks), dma((2,)), dma((2,)),
         ],
         compiler_params=pltpu.CompilerParams(
-            collective_id=0, has_side_effects=True, vmem_limit_bytes=58 * 1024 * 1024),
-    )(ans_len, prompt_len, q_ans, kv_ans, q_prompt, kv_prompt, dout_ans, dout_prompt)
+            collective_id=1, has_side_effects=True, vmem_limit_bytes=58 * 1024 * 1024),
+    )(terms)
+    return d_q_ans, d_kv_ans, d_q_prompt, d_kv_prompt
 
 
 def solution(mesh):

time: 80.5 us -> 93.3 us (1.16)
  Pallas kernels: 74.1 us -> 89.2 us
  local copies, waits for them, and re-layouts: 4 us -> 1.38 us
    pallas_call x1 -> x3, Pallas kernels: 74.1 us -> 89.2 us  [the longest x1 39.8 us: per_device(): pl.pallas_call(functools.partial(gather, nz), out_shape=jax.ShapeDtypeStr...]
    unnamed x10 -> x1, local copies, waits for them, and re-layouts: 4 us -> 1.38 us
where the time goes in v2:
time: 93.3 us; the launch traced here: 92.5 us
  Pallas kernels  89.2 us (96%)
  between operations  1.95 us (2%)
  local copies, waits for them, and re-layouts  1.38 us (1%)
    pallas_call x1, Pallas kernels, per_device(): pl.pallas_call(functools.partial(gather, nz), out_shape=jax.ShapeDtypeStr...  39.8 us
    pallas_call x1, Pallas kernels, per_device(): pl.pallas_call(functools.partial(scatter, nz), out_shape=jax.ShapeDtypeSt...  32.7 us
    pallas_call x1, Pallas kernels, per_device(): pl.pallas_call(functools.partial(attend, nz), out_shape=(jax.ShapeDtypeSt...  16.7 us

profile of v2, /device:TPU:24, one launch (start us, length us, event | category | flops | bytes accessed | tf_op | source)
XLA Modules:
  0.0 92.5 jit_solution(11165490009560060790)
XLA Ops:
  1.9 39.8 %shard_map.111.kv_all = bf16[2,2176,128]{2,1,0:T(8,128)(2,1)} custom-call(bf16[2,64,128]{2,1,0:T(8,128)(2,1)} %kv_p.1), custom_call_target="tpu_custom_call" | custom-call | tf_op jit(solution)/shard_map/pallas_call | solution.py:351
  41.8 16.7 %shard_map.112 = (bf16[128,1024]{1,0:T(8,128)(2,1)}, bf16[2,128,128]{2,1,0:T(8,128)(2,1)}, bf16[64,1024]{1,0:T(8,128)(2,1)}, f32[2,2176,128]{2,1,0:T(8,128)}) custom-call(s32[1]{0:T(128)S(6)} %copy.13.ans_len, s32[1]{0:T(128)S(6)} %copy.14.prompt_len, bf16[128,1024]{1,0:T(8,128)(2,1)} %q_a.1, bf16[2,128,128]{2,1,0:T(8,128)(2,1)} %kv_a.1, ...), custom_call_target="tpu_custom_call" | custom-call | tf_op jit(solution)/shard_map/pallas_call | solution.py:363
  58.5 32.7 %shard_map.113 = bf16[2,64,128]{2,1,0:T(8,128)(2,1)} custom-call(f32[2,2176,128]{2,1,0:T(8,128)} %get-tuple-element.11.terms_in), custom_call_target="tpu_custom_call" | custom-call | tf_op jit(solution)/shard_map/pallas_call | solution.py:394
  91.2 1.4 %copy.15 = bf16[2,64,128]{2,1,0:T(8,128)(2,1)} copy(bf16[2,64,128]{2,1,0:T(8,128)(2,1)} %shard_map.113) | data formatting | bytes 65536

commit v3 on v1

--- a/solution.py
+++ b/solution.py
@@ -53,56 +53,44 @@
         pltpu.make_async_copy(g_p.at[:, cols], g.at[pl.ds(A_ROWS + h * PIECE, PIECE)], ld_sem.at[1]).start()
     own_row = pl.multiple_of(par * PIECE, PIECE)
     cross_row = pl.multiple_of((1 - par) * PIECE, PIECE)
-    own_load = pltpu.make_async_copy(kv_p, kv.at[:, pl.ds(own_row, PIECE)], ld_sem.at[2])
-    own_load.start()
-    ans_load = pltpu.make_async_copy(kv_a, kv.at[:, pl.ds(128, ALEN)], ld_sem.at[3])
-    ans_load.start()
+    loads = [pltpu.make_async_copy(kv_p, kv.at[par], ld_sem.at[2])]
+    for i in range(2):
+        rows = pl.ds(i * PIECE, PIECE)
+        loads.append(pltpu.make_async_copy(kv_a.at[:, rows], kv.at[2 + i], ld_sem.at[3 + i]))
+    for load in loads:
+        load.start()
 
     barrier = pltpu.get_barrier_semaphore()
     for peer in (right, left, cross):
         pl.semaphore_signal(barrier, inc=1, device_id={"ans": peer}, device_id_type=MESH)
     pl.semaphore_wait(barrier, 3)
 
-    def block_row(s, d, r):
-        return pl.multiple_of(s * 256 + d * 128 + r * PIECE, PIECE)
-
-    def hop(s, d, c, r, src=None):
+    def hop(s, d, r, src=None):
         first = isinstance(s, int) and s == 1
         last = isinstance(s, int) and s == half
         if src is None:
-            row = pl.multiple_of(r * PIECE, PIECE) if first else block_row(s - 1, d, r)
-            src = kv.at[c, pl.ds(row, PIECE)]
-        row = 256 * half + r * PIECE if last else block_row(s, d, r)
+            src = kv.at[r if first else 4 * (s - 1) + 2 * d + r]
         return pltpu.make_async_remote_copy(
-            src_ref=src, dst_ref=kv.at[c, pl.ds(row, PIECE)],
-            send_sem=ag_send.at[d, c, r], recv_sem=ag_recv.at[s - 1, d, c, r],
+            src_ref=src, dst_ref=kv.at[4 * half + r if last else 4 * s + 2 * d + r],
+            send_sem=ag_send.at[d, r], recv_sem=ag_recv.at[s - 1, d, r],
             device_id=towards(d), device_id_type=MESH)
 
-    def exchange(c):
+    def exchange(slot):
         return pltpu.make_async_remote_copy(
-            src_ref=kv_p.at[c], dst_ref=kv.at[c, pl.ds(own_row, PIECE)],
-            send_sem=gx_send.at[c], recv_sem=gx_recv.at[c],
+            src_ref=kv_p, dst_ref=kv.at[slot], send_sem=gx_send, recv_sem=gx_recv,
             device_id={"ans": cross}, device_id_type=MESH)
 
-    def arrival(c):
-        return pltpu.make_async_remote_copy(
-            src_ref=kv_p.at[c], dst_ref=kv.at[c, pl.ds(cross_row, PIECE)],
-            send_sem=gx_send.at[c], recv_sem=gx_recv.at[c],
-            device_id={"ans": cross}, device_id_type=MESH)
-
-    for c in range(2):
-        exchange(c).start()
-        for d in range(2):
-            hop(1, d, c, par, kv_p.at[c]).start()
-    for c in range(2):
-        arrival(c).wait_recv()
-        for d in range(2):
-            hop(1, d, c, 1 - par).start()
+    exchange(par).start()
+    for d in range(2):
+        hop(1, d, par, kv_p).start()
+    exchange(1 - par).wait_recv()
+    for d in range(2):
+        hop(1, d, 1 - par).start()
 
     pltpu.make_async_copy(q, q, ld_sem.at[0]).wait()
     pltpu.make_async_copy(g, g, ld_sem.at[1]).wait()
-    own_load.wait()
-    ans_load.wait()
+    for load in loads:
+        load.wait()
     tok = lax.broadcasted_iota(jnp.int32, (A_ROWS, HD), 0) & (ALEN - 1)
     g[0:A_ROWS] = jnp.where(tok < alen, g[0:A_ROWS], jnp.zeros((), BF16))
     tok = me * PIECE + (lax.broadcasted_iota(jnp.int32, (P_ROWS, HD), 0) & (PIECE - 1))
@@ -118,8 +106,9 @@
     def score_group(s, off, bases, own):
         n = PIECE * len(bases) + (ALEN if own else 0)
         rows = pl.ds(off, n)
-        keys = kv[0, rows, :]
-        values = kv[1, rows, :]
+        slots = pl.ds(4 * s, n // PIECE)
+        keys = kv[slots, 0].reshape(n, HD)
+        values = kv[slots, 1].reshape(n, HD)
         for j in range(CHUNKS):
             lanes = slice(j * LANES, (j + 1) * LANES)
             lim, lim_own = limits(j)
@@ -155,36 +144,33 @@
 
     score_group(0, 0, [base_of(0, 0, 0), base_of(0, 0, 1)], True)
 
+    def pass_on(s):
+        for r in (par, 1 - par):
+            for d in range(2):
+                hop(s, d, r).wait()
+                hop(s + 1, d, r).start()
+
+    def four(s):
+        return [base_of(s, d, r) for d in range(2) for r in range(2)]
+
     def middle(s, carry):
-        for r in (par, 1 - par):
-            for c in range(2):
-                for d in range(2):
-                    hop(s, d, c, r).wait()
-                    hop(s + 1, d, c, r).start()
-        score_group(s, pl.multiple_of(s * 256, 256),
-                    [base_of(s, d, r) for d in range(2) for r in range(2)], False)
+        pass_on(s)
+        score_group(s, pl.multiple_of(s * 256, 256), four(s), False)
         return carry
 
-    for r in (par, 1 - par):
-        for c in range(2):
-            for d in range(2):
-                hop(1, d, c, r).wait()
-                hop(2, d, c, r).start()
-    score_group(1, 256, [base_of(1, d, r) for d in range(2) for r in range(2)], False)
+    pass_on(1)
+    score_group(1, 256, four(1), False)
     lax.fori_loop(2, half - 1, middle, 0)
     s = half - 1
     for r in range(2):
-        for c in range(2):
-            for d in range(2):
-                hop(s, d, c, r).wait()
-                if r == d:
-                    hop(half, d, c, r).start()
-    score_group(s, s * 256, [base_of(s, d, r) for d in range(2) for r in range(2)], False)
-    for c in range(2):
         for d in range(2):
-            hop(half, d, c, d).wait()
-    for c in range(2):
-        exchange(c).wait_send()
+            hop(s, d, r).wait()
+            if r == d:
+                hop(half, d, r).start()
+    score_group(s, s * 256, four(s), False)
+    for d in range(2):
+        hop(half, d, d).wait()
+    exchange(par).wait_send()
     score_group(half, half * 256, [base_of(half, d, d) for d in range(2)], False)
 
     m8 = mrun[...]
@@ -227,15 +213,18 @@
         if first >= last:
             lax.fori_loop(0, first - last + 1, lambda i, carry: (fn(first - i), carry)[1], 0)
 
-    def partial_sum(far, d, c, r):
+    def partial_sum(far, d, c):
+        part = pl.ds(d, 1) if far == half else pl.ds(0, 2)
         return pltpu.make_async_remote_copy(
-            src_ref=rs_out.at[far - 1, d, c, r], dst_ref=rs_in.at[far - 1, d, c, r],
-            send_sem=rs_send.at[d, c, r], recv_sem=rs_recv.at[far - 1, d, c, r],
+            src_ref=rs_out.at[far - 1, d, c, part], dst_ref=rs_in.at[far - 1, d, c, part],
+            send_sem=rs_send.at[d, c], recv_sem=rs_recv.at[far - 1, d, c],
             device_id=towards(d), device_id_type=MESH)
 
     def ring(c, far):
-        for r in range(2):
-            for d in range(2):
+        for d in range(2):
+            if far < half:
+                partial_sum(far + 1, d, c).wait()
+            for r in range(2):
                 if far == half:
                     if r != d:
                         continue
@@ -244,10 +233,9 @@
                     row = far * 256 + (1 - d) * 128 + r * PIECE
                 term = terms[c, row:row + PIECE, :]
                 if far < half - 1 or (far == half - 1 and r == d):
-                    partial_sum(far + 1, d, c, r).wait()
                     term = term + rs_in[far, d, c, r].astype(F32)
                 rs_out[far - 1, d, c, r] = term.astype(BF16)
-                partial_sum(far, d, c, r).start()
+            partial_sum(far, d, c).start()
 
     def swap(c):
         return pltpu.make_async_remote_copy(
@@ -258,11 +246,12 @@
     def gathered_sum(c, row, r):
         acc = terms[c, pl.ds(row, PIECE), :]
         for d in range(2):
-            partial_sum(1, d, c, r).wait()
             acc = acc + rs_in[0, d, c, r].astype(F32)
         return acc
 
     def finish(c):
+        for d in range(2):
+            partial_sum(1, d, c).wait()
         x_out[c] = gathered_sum(c, cross_row, 1 - par).astype(BF16)
         swap(c).start()
         terms[c, pl.ds(own_row, PIECE), :] = gathered_sum(c, own_row, par)
@@ -297,7 +286,7 @@
             finish(V)
     own_out[...] = terms[:, 128:256, :].astype(BF16)
     for s in range(n_keys // 128):
-        kt[:, s * 128:(s + 1) * 128] = kv[0, s * 128:(s + 1) * 128, :].T
+        kt[:, s * 128:(s + 1) * 128] = kv[2 * s:2 * s + 2, 0].reshape(128, HD).T
     for j in range(CHUNKS):
         query_terms(j)
         if j % 2 == 1:
@@ -346,7 +335,7 @@
         in_specs=[smem, smem] + [any_spec] * 6,
         out_specs=(any_spec,) * 4,
         scratch_shapes=[
-            vm((2, n_keys, HD), BF16),
+            vm((n_keys // PIECE, 2, PIECE, HD), BF16),
             vm((HD, n_keys), BF16),
             vm((ROWS, HD), BF16),
             vm((ROWS, HD), BF16),
@@ -367,9 +356,9 @@
             vm(blocks + (PIECE, HD), BF16),
             vm((2, PIECE, HD), BF16),
             vm((2, PIECE, HD), BF16),
-            dma((4,)), dma((3,)),
-            dma((2, 2, 2)), dma(blocks), dma((2,)), dma((2,)),
-            dma((2, 2, 2)), dma(blocks), dma((2,)), dma((2,)),
+            dma((5,)), dma((3,)),
+            dma((2, 2)), dma((half, 2, 2)), dma(()), dma(()),
+            dma((2, 2)), dma((half, 2, 2)), dma((2,)), dma((2,)),
         ],
         compiler_params=pltpu.CompilerParams(
             collective_id=0, has_side_effects=True, vmem_limit_bytes=58 * 1024 * 1024),

time: 80.5 us -> 80.8 us (level)
  no operation moved by 1% of the time
where the time goes in v3:
time: 80.8 us; the launch traced here: 80.6 us
  Pallas kernels  74.6 us (92%)
  local copies, waits for them, and re-layouts  4 us (5%)
  between operations  1.94 us (2%)
    pallas_call x1, Pallas kernels, per_device(): pl.pallas_call(functools.partial(kernel, nz), out_shape=(jax.ShapeDtypeSt...  74.6 us
    unnamed x10, local copies, waits for them, and re-layouts  4 us

profile of v3, /device:TPU:24, one launch (start us, length us, event | category | flops | bytes accessed | tf_op | source)
XLA Modules:
  0.0 80.6 jit_solution(9277397760376427565)
XLA Ops:
  1.9 74.6 %shard_map.111 = (bf16[128,1024]{1,0:T(8,128)(2,1)}, bf16[2,128,128]{2,1,0:T(8,128)(2,1)}, bf16[64,1024]{1,0:T(8,128)(2,1)}, bf16[2,64,128]{2,1,0:T(8,128)(2,1)}) custom-call(s32[1]{0:T(128)S(6)} %copy.16.ans_len, s32[1]{0:T(128)S(6)} %copy.17.prompt_len, bf16[128,1024]{1,0:T(8,128)(2,1)} %q_a.1, bf16[2,128,128]{2,1,0:T(8,128)(2,1)} %kv_a.1, ...), custom_call_target="tpu_custom_call" | custom-call | tf_op jit(solution)/shard_map/pallas_call | solution.py:327
  76.5 0.0 copy-start.1
  76.6 1.7 %copy.18 = bf16[128,1024]{1,0:T(8,128)(2,1)} copy(bf16[128,1024]{1,0:T(8,128)(2,1)} %get-tuple-element.8) | data formatting | bytes 524288
  78.3 0.0 copy-done.1
  78.3 0.0 copy-start
  78.3 0.6 copy.19
  78.9 0.3 copy-done
  79.2 0.0 copy-start.2
  79.2 0.7 copy.20
  79.8 0.1 copy-done.2
  79.9 0.6 copy.21
Async XLA Ops:
  76.5 1.7 %copy-start.1 = (bf16[2,128,128]{2,1,0:T(8,128)(2,1)S(1)}, bf16[2,128,128]{2,1,0:T(8,128)(2,1)}, u32[]{:S(2)}) copy-start(bf16[2,128,128]{2,1,0:T(8,128)(2,1)} %get-tuple-element.9) | copy-start | bytes 196612
  78.3 0.9 %copy-start = (bf16[64,1024]{1,0:T(8,128)(2,1)S(1)}, bf16[64,1024]{1,0:T(8,128)(2,1)}, u32[]{:S(2)}) copy-start(bf16[64,1024]{1,0:T(8,128)(2,1)} %get-tuple-element.10) | copy-start | bytes 393220
  79.2 0.8 copy-start.2

commit v4 on v3

v4 whole, which is shorter than its diff:
```python
import functools
import math

import jax
import jax.numpy as jnp
from jax import lax
from jax.experimental import pallas as pl
from jax.experimental.pallas import tpu as pltpu
from jax.sharding import PartitionSpec as P

MESH = pl.DeviceIdType.MESH
F32, BF16 = jnp.float32, jnp.bfloat16
HD = 128
HEADS = 8
ALEN = 128
PIECE = 64
A_ROWS = HEADS * ALEN
P_ROWS = HEADS * PIECE
ROWS = A_ROWS + P_ROWS
LANES = 256
CHUNKS = ROWS // LANES
SCALE = 1.0 / math.sqrt(HD)
COEF = SCALE * math.log2(math.e)
NEG = -1e30
NT = (((1,), (1,)), ((), ()))


NEAR = (0, 1, -1, 2)


def kernel(nz, ans_len, prompt_len, q_a, kv_a, q_p, kv_p, g_a, g_p,
           dq_a, dkv_a, dq_p, dkv_p,
           kv, kt, q, g, e, dp, ds, pbuf, mrun, tot, mgrp, rgrp, delta,
           terms, dq, own_out, prm_out,
           x_out, x_in, near_out, near_in, far_out, far_in,
           ld_sem, st_sem, gf_send, gf_recv, gn_send, gn_recv, gx_send, gx_recv,
           sf_send, sf_recv, sn_send, sn_recv, sx_send, sx_recv):
    fars = nz // 4
    last = 2 * fars
    n_keys = 256 * last + 128
    alen = ans_len[0]
    plen = prompt_len[0]
    me = lax.axis_index("ans")
    side = 1 - 2 * (lax.axis_index("group") % 2)
    par = me // nz
    z = me % nz
    cross = {"ans": (1 - par) * nz + z}

    def along(step):
        return (z + side * step + 2 * nz) % nz

    def peer(step):
        return {"ans": par * nz + along(step)}

    barrier = pltpu.get_barrier_semaphore()
    steps = sorted({n % nz for n in (1, -1, 2, -2)} | {4 * f for f in range(1, fars)})
    for other in [peer(step) for step in steps] + [cross]:
        pl.semaphore_signal(barrier, inc=1, device_id=other, device_id_type=MESH)

    loads = [pltpu.make_async_copy(kv_p, kv.at[0], ld_sem.at[2])]
    for i in range(2):
        rows = pl.ds(i * PIECE, PIECE)
        loads.append(pltpu.make_async_copy(kv_a.at[:, rows], kv.at[4 * last + i], ld_sem.at[3 + i]))
    for load in loads:
        load.start()
    for h in range(HEADS):
        cols = pl.ds(h * HD, HD)
        pltpu.make_async_copy(q_a.at[:, cols], q.at[pl.ds(h * ALEN, ALEN)], ld_sem.at[0]).start()
        pltpu.make_async_copy(q_p.at[:, cols], q.at[pl.ds(A_ROWS + h * PIECE, PIECE)], ld_sem.at[0]).start()
        pltpu.make_async_copy(g_a.at[:, cols], g.at[pl.ds(h * ALEN, ALEN)], ld_sem.at[1]).start()
        pltpu.make_async_copy(g_p.at[:, cols], g.at[pl.ds(A_ROWS + h * PIECE, PIECE)], ld_sem.at[1]).start()

    pl.semaphore_wait(barrier, len(steps) + 1)

    def remote(src, dst, send, recv, device):
        return pltpu.make_async_remote_copy(
            src_ref=src, dst_ref=dst, send_sem=send, recv_sem=recv,
            device_id=device, device_id_type=MESH)

    def to_far(f):
        return remote(kv_p, kv.at[8 * f], gf_send.at[f], gf_recv.at[f], peer(4 * f))

    def to_near(f, n, src=None):
        return remote(kv.at[8 * f] if src is None else src, kv.at[8 * f + n],
                      gn_send.at[f, n], gn_recv.at[f, n], peer(NEAR[n]))

    def to_cross(f, n, src=None):
        return remote(kv.at[8 * f + n] if src is None else src, kv.at[8 * f + 4 + n],
                      gx_send.at[f, n], gx_recv.at[f, n], cross)

    for f in range(1, fars):
        to_far(f).start()
    for n in range(1, 4):
        to_near(0, n, kv_p).start()
    to_cross(0, 0, kv_p).start()

    pltpu.make_async_copy(q, q, ld_sem.at[0]).wait()
    pltpu.make_async_copy(g, g, ld_sem.at[1]).wait()
    for load in loads:
        load.wait()
    tok = lax.broadcasted_iota(jnp.int32, (A_ROWS, HD), 0) & (ALEN - 1)
    g[0:A_ROWS] = jnp.where(tok < alen, g[0:A_ROWS], jnp.zeros((), BF16))
    tok = me * PIECE + (lax.broadcasted_iota(jnp.int32, (P_ROWS, HD), 0) & (PIECE - 1))
    g[A_ROWS:ROWS] = jnp.where(tok < plen, g[A_ROWS:ROWS], jnp.zeros((), BF16))

    def rows_of(s):
        return pl.multiple_of(s * 256, 256) if not isinstance(s, int) else s * 256

    def limits(j):
        lane = lax.broadcasted_iota(jnp.int32, (1, LANES), 1)
        if j * LANES < A_ROWS:
            return jnp.zeros((1, LANES), jnp.int32) + (plen - 1), lane & (ALEN - 1)
        pos = me * PIECE + (lane & (PIECE - 1))
        return jnp.minimum(pos, plen - 1), jnp.full((1, LANES), -1, jnp.int32)

    def score_group(s, bases, own=False):
        n = PIECE * len(bases) + (ALEN if own else 0)
        rows = pl.ds(rows_of(s), n)
        slots = pl.ds(4 * s, n // PIECE)
        keys = kv[slots, 0].reshape(n, HD)
        values = kv[slots, 1].reshape(n, HD)
        for j in range(CHUNKS):
            lanes = slice(j * LANES, (j + 1) * LANES)
            lim, lim_own = limits(j)
            raw = lax.dot_general(keys, q[lanes, :], NT, preferred_element_type=F32)
            parts = []
            for b, base in enumerate(bases):
                pos = base + lax.broadcasted_iota(jnp.int32, (PIECE, LANES), 0)
                parts.append(jnp.where(pos <= lim, raw[b * PIECE:(b + 1) * PIECE], NEG))
            if own:
                pos = lax.broadcasted_iota(jnp.int32, (ALEN, LANES), 0)
                parts.append(jnp.where(pos <= lim_own, raw[n - ALEN:n], NEG))
            raw = jnp.concatenate(parts, 0).reshape(n // 8, 8, LANES)
            high = jnp.max(raw, axis=0)
            if own:
                new = high
            else:
                old = mrun[:, lanes]
                new = jnp.maximum(old, high)
            ex = jnp.exp2((raw - new[None]) * COEF)
            part = jnp.sum(ex, axis=0)
            if own:
                tot[:, lanes] = part
            else:
                tot[:, lanes] = tot[:, lanes] * jnp.exp2((old - new) * COEF) + part
            mrun[:, lanes] = new
            mgrp[s, :, lanes] = new
            e[rows, lanes] = ex.reshape(n, LANES)
            dp[rows, lanes] = lax.dot_general(values, g[lanes, :], NT, preferred_element_type=F32)

    def bases(f, k):
        half = par if k == 0 else 1 - par
        return [(half * nz + along(-(NEAR[n] + 4 * f))) * PIECE for n in range(4)]

    score_group(last, [], True)
    for f in range(1, fars):
        to_far(f).wait_recv()
        for n in range(1, 4):
            to_near(f, n).start()
        to_cross(f, 0).start()

    def this_half(f, carry):
        for n in range(1, 4):
            to_near(f, n).wait_recv()
            to_cross(f, n).start()
        score_group(2 * f, bases(f, 0))
        return carry

    def other_half(f, carry):
        for n in range(4):
            to_cross(f, n).wait_recv()
        score_group(2 * f + 1, bases(f, 1))
        return carry

    lax.fori_loop(0, fars, this_half, 0)
    lax.fori_loop(0, fars, other_half, 0)

    m8 = mrun[...]
    top = jnp.max(m8, axis=0, keepdims=True)
    total = jnp.sum(tot[...] * jnp.exp2((m8 - top) * COEF), axis=0, keepdims=True)
    inv = 1.0 / total
    for s in range(last + 1):
        rgrp[s] = jnp.exp2((mgrp[s] - top) * COEF) * inv
    delta[...] = jnp.zeros_like(delta)

    def value_terms(s, n=256):
        rows = pl.ds(rows_of(s), n)
        for j in range(CHUNKS):
            lanes = slice(j * LANES, (j + 1) * LANES)
            p = e[rows, lanes].reshape(n // 8, 8, LANES) * rgrp[s, :, lanes][None]
            pb = p.reshape(n, LANES).astype(BF16)
            pbuf[0:n, lanes] = pb
            prod = pb.astype(F32) * dp[rows, lanes]
            delta[:, lanes] += jnp.sum(prod.reshape(n // 8, 8, LANES), axis=0)
        terms[1, rows, :] = jnp.dot(pbuf[0:n], g[...], preferred_element_type=F32)

    def key_terms(s, n=256):
        rows = pl.ds(rows_of(s), n)
        for j in range(CHUNKS):
            lanes = slice(j * LANES, (j + 1) * LANES)
            p = e[rows, lanes].reshape(n // 8, 8, LANES) * (rgrp[s, :, lanes] * SCALE)[None]
            diff = dp[rows, lanes].reshape(n // 8, 8, LANES) - delta[:, lanes][None]
            ds[rows, lanes] = (p * diff).reshape(n, LANES).astype(BF16)
        terms[0, rows, :] = jnp.dot(ds[rows, :], q[...], preferred_element_type=F32)

    def query_terms(j):
        lanes = slice(j * LANES, (j + 1) * LANES)
        flipped = jnp.dot(kt[...], ds[:, lanes], preferred_element_type=F32)
        dq[lanes, :] = flipped.T.astype(BF16)

    def sum_cross(c, f):
        return remote(x_out.at[c, f], x_in.at[c, f], sx_send.at[c, f], sx_recv.at[c, f], cross)

    def sum_near(c, f, n):
        return remote(near_out.at[c, f, n - 1], near_in.at[c, f, n - 1],
                      sn_send.at[c, f, n - 1], sn_recv.at[c, f, n - 1], peer(-NEAR[n]))

    def sum_far(c, f):
        return remote(far_out.at[c, f - 1], far_in.at[c, f - 1],
                      sf_send.at[c, f - 1], sf_recv.at[c, f - 1], peer(-4 * f))

    def send_cross(c, f):
        x_out[c, f] = terms[c, pl.ds(rows_of(2 * f + 1), 256), :].astype(BF16)
        sum_cross(c, f).start()

    def send_near(c, f):
        sum_cross(c, f).wait_recv()
        row = 512 * f
        for n in range(1, 4):
            part = terms[c, row + n * PIECE:row + (n + 1) * PIECE, :]
            part = part + x_in[c, f, n * PIECE:(n + 1) * PIECE, :].astype(F32)
            near_out[c, f, n - 1] = part.astype(BF16)
            sum_near(c, f, n).start()

    def held(c, f):
        row = 512 * f
        acc = terms[c, row:row + PIECE, :] + x_in[c, f, 0:PIECE, :].astype(F32)
        for n in range(1, 4):
            sum_near(c, f, n).wait_recv()
            acc = acc + near_in[c, f, n - 1].astype(F32)
        return acc

    def send_far(c, f):
        far_out[c, f - 1] = held(c, f).astype(BF16)
        sum_far(c, f).start()

    def finish(c):
        acc = held(c, 0)
        for f in range(1, fars):
            sum_far(c, f).wait_recv()
            acc = acc + far_in[c, f - 1].astype(F32)
        prm_out[c] = acc.astype(BF16)

    K, V = 0, 1

    def value_cross(i, carry):
        f = fars - 1 - i
        value_terms(2 * f + 1)
        send_cross(V, f)
        return carry

    def key_cross(i, carry):
        f = fars - 1 - i
        key_terms(2 * f + 1)
        send_cross(K, f)
        return carry

    lax.fori_loop(0, fars, value_cross, 0)
    value_terms(last, 128)
    lax.fori_loop(0, fars, lambda i, carry: (value_terms(2 * (fars - 1 - i)), carry)[1], 0)
    delta[...] = jnp.broadcast_to(jnp.sum(delta[...], axis=0, keepdims=True), delta.shape)
    lax.fori_loop(0, fars, key_cross, 0)
    for f in range(fars - 1, fars // 2 - 1, -1):
        send_near(V, f)
    lax.fori_loop(0, fars // 2, lambda i, carry: (key_terms(2 * (fars - 1 - i)), carry)[1], 0)
    for f in range(fars // 2 - 1, -1, -1):
        send_near(V, f)
    lax.fori_loop(fars // 2, fars, lambda i, carry: (key_terms(2 * (fars - 1 - i)), carry)[1], 0)
    key_terms(last, 128)
    own_out[...] = terms[:, 256 * last:256 * last + ALEN, :].astype(BF16)
    own_store = pltpu.make_async_copy(own_out, dkv_a, st_sem.at[0])
    own_store.start()
    for s in range(n_keys // 128):
        kt[:, s * 128:(s + 1) * 128] = kv[2 * s:2 * s + 2, 0].reshape(128, HD).T
    query_terms(0)
    query_terms(1)
    todo_near = list(range(fars - 1, -1, -1))
    todo_far = list(range(fars - 1, 0, -1))
    for f in todo_far:
        send_far(V, f)
    send_near(K, todo_near.pop(0))
    query_terms(2)
    query_terms(3)
    send_near(K, todo_near.pop(0))
    query_terms(4)
    query_terms(5)
    for h in range(HEADS):
        cols = pl.ds(h * HD, HD)
        pltpu.make_async_copy(dq.at[pl.ds(h * ALEN, ALEN)], dq_a.at[:, cols], st_sem.at[1]).start()
        pltpu.make_async_copy(dq.at[pl.ds(A_ROWS + h * PIECE, PIECE)], dq_p.at[:, cols], st_sem.at[1]).start()
    for f in todo_near:
        send_near(K, f)
    for f in todo_far:
        send_far(K, f)
    finish(V)
    finish(K)
    out = pltpu.make_async_copy(prm_out, dkv_p, st_sem.at[2])
    out.start()

    for f in range(fars):
        for n in range(4):
            to_cross(f, n).wait_send()
            if n:
                to_near(f, n).wait_send()
        if f:
            to_far(f).wait_send()
        for c in range(2):
            sum_cross(c, f).wait_send()
            for n in range(1, 4):
                sum_near(c, f, n).wait_send()
            if f:
                sum_far(c, f).wait_send()
    own_store.wait()
    pltpu.make_async_copy(dq, dq, st_sem.at[1]).wait()
    out.wait()


def deliver(*refs):
    sems = refs[-1]
    count = len(refs) // 2
    copies = [pltpu.make_async_copy(refs[i], refs[count + i], sems.at[i]) for i in range(count)]
    for copy in copies:
        copy.start()
    for copy in copies:
        copy.wait()


def per_device(nz, q_ans, kv_ans, q_prompt, kv_prompt, dout_ans, dout_prompt, ans_len, prompt_len):
    fars = nz // 4
    groups = 2 * fars + 1
    n_keys = 512 * fars + 128
    any_spec = pl.BlockSpec(memory_space=pl.ANY)
    smem = pl.BlockSpec(memory_space=pltpu.SMEM)
    dma, vm = pltpu.SemaphoreType.DMA, pltpu.VMEM
    out_shape = tuple(jax.ShapeDtypeStruct(a.shape, BF16) for a in (q_ans, kv_ans, q_prompt, kv_prompt))
    results = pl.pallas_call(
        functools.partial(kernel, nz),
        out_shape=out_shape,
        in_specs=[smem, smem] + [any_spec] * 6,
        out_specs=(any_spec,) * 4,
        scratch_shapes=[
            vm((n_keys // PIECE, 2, PIECE, HD), BF16),
            vm((HD, n_keys), BF16),
            vm((ROWS, HD), BF16),
            vm((ROWS, HD), BF16),
            vm((n_keys, ROWS), F32),
            vm((n_keys, ROWS), F32),
            vm((n_keys, ROWS), BF16),
            vm((256, ROWS), BF16),
            vm((8, ROWS), F32),
            vm((8, ROWS), F32),
            vm((groups, 8, ROWS), F32),
            vm((groups, 8, ROWS), F32),
            vm((8, ROWS), F32),
            vm((2, n_keys, HD), F32),
            vm((ROWS, HD), BF16),
            vm((2, ALEN, HD), BF16),
            vm((2, PIECE, HD), BF16),
            vm((2, fars, 256, HD), BF16), vm((2, fars, 256, HD), BF16),
            vm((2, fars, 3, PIECE, HD), BF16), vm((2, fars, 3, PIECE, HD), BF16),
            vm((2, fars - 1, PIECE, HD), BF16), vm((2, fars - 1, PIECE, HD), BF16),
            dma((5,)), dma((3,)),
            dma((fars,)), dma((fars,)), dma((fars, 4)), dma((fars, 4)), dma((fars, 4)), dma((fars, 4)),
            dma((2, fars - 1)), dma((2, fars - 1)), dma((2, fars, 3)), dma((2, fars, 3)),
            dma((2, fars)), dma((2, fars)),
        ],
        compiler_params=pltpu.CompilerParams(
            collective_id=0, has_side_effects=True, vmem_limit_bytes=58 * 1024 * 1024),
    )(ans_len, prompt_len, q_ans, kv_ans, q_prompt, kv_prompt, dout_ans, dout_prompt)
    return pl.pallas_call(
        deliver, out_shape=out_shape, in_specs=[any_spec] * 4, out_specs=(any_spec,) * 4,
        scratch_shapes=[dma((4,))],
    )(*results)


def solution(mesh):
    in_specs = (
        P(("group", "ans"), "tp"),
        P(None, ("group", "ans"), "tp"),
        P(("group", "ans"), "tp"),
        P(None, ("group", "ans"), "tp"),
        P(("group", "ans"), "tp"),
        P(("group", "ans"), "tp"),
        P(("group", "ans")),
        P("group"),
    )
    out_specs = (
        P(("group", "ans"), "tp"),
        P(None, ("group", "ans"), "tp"),
        P(("group", "ans"), "tp"),
        P(None, ("group", "ans"), "tp"),
    )
    return jax.shard_map(
        functools.partial(per_device, mesh.shape["ans"] // 2), mesh=mesh,
        in_specs=in_specs, out_specs=out_specs, check_vma=False)
```

time: 80.8 us -> 81.9 us (1.014)
  Pallas kernels: 74.6 us -> 79.9 us
  local copies, waits for them, and re-layouts: 4 us -> 0 us
    pallas_call x1 -> x2, Pallas kernels: 74.6 us -> 79.9 us  [the longest x1 63.8 us: per_device(): pl.pallas_call(functools.partial(kernel, nz), out_shape=out_shape, in_spe...]
    unnamed x10 -> x0, local copies, waits for them, and re-layouts: 4 us -> none
where the time goes in v4:
time: 81.9 us; the launch traced here: 81.8 us
  Pallas kernels  79.9 us (98%)
  between operations  1.93 us (2%)
    pallas_call x1, Pallas kernels, per_device(): pl.pallas_call(functools.partial(kernel, nz), out_shape=out_shape, in_spe...  63.8 us
    pallas_call x1, Pallas kernels, per_device(): pl.pallas_call(deliver, out_shape=out_shape, in_specs=[any_spec] * 4, out...  16 us

profile of v4, /device:TPU:24, one launch (start us, length us, event | category | flops | bytes accessed | tf_op | source)
XLA Modules:
  0.0 81.8 jit_solution(16628556104389001238)
XLA Ops:
  1.9 63.8 %shard_map.111 = (bf16[128,1024]{1,0:T(8,128)(2,1)}, bf16[2,128,128]{2,1,0:T(8,128)(2,1)}, bf16[64,1024]{1,0:T(8,128)(2,1)}, bf16[2,64,128]{2,1,0:T(8,128)(2,1)}) custom-call(s32[1]{0:T(128)S(6)} %copy.12.ans_len, s32[1]{0:T(128)S(6)} %copy.13.prompt_len, bf16[128,1024]{1,0:T(8,128)(2,1)} %q_a.1, bf16[2,128,128]{2,1,0:T(8,128)(2,1)} %kv_a.1, ...), custom_call_target="tpu_custom_call" | custom-call | tf_op jit(solution)/shard_map/pallas_call | solution.py:346
  65.8 16.0 %shard_map.112 = (bf16[128,1024]{1,0:T(8,128)(2,1)}, bf16[2,128,128]{2,1,0:T(8,128)(2,1)}, bf16[64,1024]{1,0:T(8,128)(2,1)}, bf16[2,64,128]{2,1,0:T(8,128)(2,1)}) custom-call(bf16[128,1024]{1,0:T(8,128)(2,1)} %get-tuple-element.8.refs_0_, bf16[2,128,128]{2,1,0:T(8,128)(2,1)} %get-tuple-element.9.refs_1_, bf16[64,1024]{1,0:T(8,128)(2,1)} %get-tuple-element.10.refs_2_, ...), custom_call_target="tpu_custom_call" | custom-call | tf_op jit(solution)/shard_map/pallas_call | solution.py:380

commit v5 on v4

--- a/solution.py
+++ b/solution.py
@@ -30,10 +30,9 @@
 
 def kernel(nz, ans_len, prompt_len, q_a, kv_a, q_p, kv_p, g_a, g_p,
            dq_a, dkv_a, dq_p, dkv_p,
-           kv, kt, q, g, e, dp, ds, pbuf, mrun, tot, mgrp, rgrp, delta,
-           terms, dq, own_out, prm_out,
+           kv, kt, q, g, e, dp, ds, mrun, tot, mgrp, rgrp, delta, terms,
            x_out, x_in, near_out, near_in, far_out, far_in,
-           ld_sem, st_sem, gf_send, gf_recv, gn_send, gn_recv, gx_send, gx_recv,
+           ld_sem, gf_send, gf_recv, gn_send, gn_recv, gx_send, gx_recv,
            sf_send, sf_recv, sn_send, sn_recv, sx_send, sx_recv):
     fars = nz // 4
     last = 2 * fars
@@ -77,22 +76,35 @@
             src_ref=src, dst_ref=dst, send_sem=send, recv_sem=recv,
             device_id=device, device_id_type=MESH)
 
-    def to_far(f):
-        return remote(kv_p, kv.at[8 * f], gf_send.at[f], gf_recv.at[f], peer(4 * f))
-
-    def to_near(f, n, src=None):
-        return remote(kv.at[8 * f] if src is None else src, kv.at[8 * f + n],
-                      gn_send.at[f, n], gn_recv.at[f, n], peer(NEAR[n]))
-
-    def to_cross(f, n, src=None):
-        return remote(kv.at[8 * f + n] if src is None else src, kv.at[8 * f + 4 + n],
-                      gx_send.at[f, n], gx_recv.at[f, n], cross)
-
+    def to_far(c, f):
+        return remote(kv_p.at[c], kv.at[8 * f, c], gf_send.at[c, f], gf_recv.at[c, f], peer(4 * f))
+
+    def to_near(c, f, n, src=None):
+        return remote(kv.at[8 * f, c] if src is None else src, kv.at[8 * f + n, c],
+                      gn_send.at[c, f, n], gn_recv.at[c, f, n], peer(NEAR[n]))
+
+    def to_cross(c, f, n, src=None):
+        return remote(kv.at[8 * f + n, c] if src is None else src, kv.at[8 * f + 4 + n, c],
+                      gx_send.at[c, f, n], gx_recv.at[c, f, n], cross)
+
+    def spread_own(c):
+        for n in range(1, 4):
+            to_near(c, 0, n, kv_p.at[c]).start()
+        to_cross(c, 0, 0, kv_p.at[c]).start()
+
+    def spread_far(c):
+        for f in range(1, fars):
+            to_far(c, f).wait_recv()
+            for n in range(1, 4):
+                to_near(c, f, n).start()
+            to_cross(c, f, 0).start()
+
+    K, V = 0, 1
     for f in range(1, fars):
-        to_far(f).start()
-    for n in range(1, 4):
-        to_near(0, n, kv_p).start()
-    to_cross(0, 0, kv_p).start()
+        to_far(K, f).start()
+    spread_own(K)
+    for f in range(1, fars):
+        to_far(V, f).start()
 
     pltpu.make_async_copy(q, q, ld_sem.at[0]).wait()
     pltpu.make_async_copy(g, g, ld_sem.at[1]).wait()
@@ -118,7 +130,6 @@
         rows = pl.ds(rows_of(s), n)
         slots = pl.ds(4 * s, n // PIECE)
         keys = kv[slots, 0].reshape(n, HD)
-        values = kv[slots, 1].reshape(n, HD)
         for j in range(CHUNKS):
             lanes = slice(j * LANES, (j + 1) * LANES)
             lim, lim_own = limits(j)
@@ -146,34 +157,39 @@
             mrun[:, lanes] = new
             mgrp[s, :, lanes] = new
             e[rows, lanes] = ex.reshape(n, LANES)
-            dp[rows, lanes] = lax.dot_general(values, g[lanes, :], NT, preferred_element_type=F32)
 
     def bases(f, k):
         half = par if k == 0 else 1 - par
         return [(half * nz + along(-(NEAR[n] + 4 * f))) * PIECE for n in range(4)]
 
     score_group(last, [], True)
-    for f in range(1, fars):
-        to_far(f).wait_recv()
-        for n in range(1, 4):
-            to_near(f, n).start()
-        to_cross(f, 0).start()
+    spread_far(K)
 
     def this_half(f, carry):
         for n in range(1, 4):
-            to_near(f, n).wait_recv()
-            to_cross(f, n).start()
+            to_near(K, f, n).wait_recv()
+            to_cross(K, f, n).start()
         score_group(2 * f, bases(f, 0))
         return carry
 
     def other_half(f, carry):
         for n in range(4):
-            to_cross(f, n).wait_recv()
+            to_cross(K, f, n).wait_recv()
         score_group(2 * f + 1, bases(f, 1))
         return carry
 
     lax.fori_loop(0, fars, this_half, 0)
+    spread_own(V)
+    spread_far(V)
     lax.fori_loop(0, fars, other_half, 0)
+
+    def values_on(f, carry):
+        for n in range(1, 4):
+            to_near(V, f, n).wait_recv()
+            to_cross(V, f, n).start()
+        return carry
+
+    lax.fori_loop(0, fars, values_on, 0)
 
     m8 = mrun[...]
     top = jnp.max(m8, axis=0, keepdims=True)
@@ -188,11 +204,18 @@
         for j in range(CHUNKS):
             lanes = slice(j * LANES, (j + 1) * LANES)
             p = e[rows, lanes].reshape(n // 8, 8, LANES) * rgrp[s, :, lanes][None]
-            pb = p.reshape(n, LANES).astype(BF16)
-            pbuf[0:n, lanes] = pb
-            prod = pb.astype(F32) * dp[rows, lanes]
+            ds[rows, lanes] = p.reshape(n, LANES).astype(BF16)
+        terms[1, rows, :] = jnp.dot(ds[rows, :], g[...], preferred_element_type=F32)
+
+    def delta_terms(s, n=256):
+        rows = pl.ds(rows_of(s), n)
+        values = kv[pl.ds(4 * s, n // PIECE), 1].reshape(n, HD)
+        for j in range(CHUNKS):
+            lanes = slice(j * LANES, (j + 1) * LANES)
+            dprob = lax.dot_general(values, g[lanes, :], NT, preferred_element_type=F32)
+            dp[rows, lanes] = dprob
+            prod = ds[rows, lanes].astype(F32) * dprob
             delta[:, lanes] += jnp.sum(prod.reshape(n // 8, 8, LANES), axis=0)
-        terms[1, rows, :] = jnp.dot(pbuf[0:n], g[...], preferred_element_type=F32)
 
     def key_terms(s, n=256):
         rows = pl.ds(rows_of(s), n)
@@ -205,8 +228,11 @@
 
     def query_terms(j):
         lanes = slice(j * LANES, (j + 1) * LANES)
-        flipped = jnp.dot(kt[...], ds[:, lanes], preferred_element_type=F32)
-        dq[lanes, :] = flipped.T.astype(BF16)
+        rows = jnp.dot(kt[...], ds[:, lanes], preferred_element_type=F32).T.astype(BF16)
+        out, tokens, first = (dq_a, ALEN, j * LANES) if j * LANES < A_ROWS else (dq_p, PIECE, j * LANES - A_ROWS)
+        for i in range(LANES // tokens):
+            head = first // tokens + i
+            out[:, head * HD:(head + 1) * HD] = rows[i * tokens:(i + 1) * tokens]
 
     def sum_cross(c, f):
         return remote(x_out.at[c, f], x_in.at[c, f], sx_send.at[c, f], sx_recv.at[c, f], cross)
@@ -249,9 +275,7 @@
         for f in range(1, fars):
             sum_far(c, f).wait_recv()
             acc = acc + far_in[c, f - 1].astype(F32)
-        prm_out[c] = acc.astype(BF16)
-
-    K, V = 0, 1
+        dkv_p[c] = acc.astype(BF16)
 
     def value_cross(i, carry):
         f = fars - 1 - i
@@ -265,21 +289,31 @@
         send_cross(K, f)
         return carry
 
+    def own_delta(f, carry):
+        delta_terms(2 * f)
+        return carry
+
+    def cross_delta(f, carry):
+        for n in range(4):
+            to_cross(V, f, n).wait_recv()
+        delta_terms(2 * f + 1)
+        return carry
+
     lax.fori_loop(0, fars, value_cross, 0)
     value_terms(last, 128)
     lax.fori_loop(0, fars, lambda i, carry: (value_terms(2 * (fars - 1 - i)), carry)[1], 0)
+    delta_terms(last, 128)
+    lax.fori_loop(0, fars, own_delta, 0)
+    lax.fori_loop(0, fars, cross_delta, 0)
     delta[...] = jnp.broadcast_to(jnp.sum(delta[...], axis=0, keepdims=True), delta.shape)
-    lax.fori_loop(0, fars, key_cross, 0)
     for f in range(fars - 1, fars // 2 - 1, -1):
         send_near(V, f)
-    lax.fori_loop(0, fars // 2, lambda i, carry: (key_terms(2 * (fars - 1 - i)), carry)[1], 0)
+    lax.fori_loop(0, fars, key_cross, 0)
     for f in range(fars // 2 - 1, -1, -1):
         send_near(V, f)
-    lax.fori_loop(fars // 2, fars, lambda i, carry: (key_terms(2 * (fars - 1 - i)), carry)[1], 0)
+    lax.fori_loop(0, fars, lambda i, carry: (key_terms(2 * (fars - 1 - i)), carry)[1], 0)
     key_terms(last, 128)
-    own_out[...] = terms[:, 256 * last:256 * last + ALEN, :].astype(BF16)
-    own_store = pltpu.make_async_copy(own_out, dkv_a, st_sem.at[0])
-    own_store.start()
+    dkv_a[...] = terms[:, 256 * last:256 * last + ALEN, :].astype(BF16)
     for s in range(n_keys // 128):
         kt[:, s * 128:(s + 1) * 128] = kv[2 * s:2 * s + 2, 0].reshape(128, HD).T
     query_terms(0)
@@ -294,35 +328,23 @@
     send_near(K, todo_near.pop(0))
     query_terms(4)
     query_terms(5)
-    for h in range(HEADS):
-        cols = pl.ds(h * HD, HD)
-        pltpu.make_async_copy(dq.at[pl.ds(h * ALEN, ALEN)], dq_a.at[:, cols], st_sem.at[1]).start()
-        pltpu.make_async_copy(dq.at[pl.ds(A_ROWS + h * PIECE, PIECE)], dq_p.at[:, cols], st_sem.at[1]).start()
     for f in todo_near:
         send_near(K, f)
     for f in todo_far:
         send_far(K, f)
     finish(V)
     finish(K)
-    out = pltpu.make_async_copy(prm_out, dkv_p, st_sem.at[2])
-    out.start()
-
-    for f in range(fars):
-        for n in range(4):
-            to_cross(f, n).wait_send()
-            if n:
-                to_near(f, n).wait_send()
-        if f:
-            to_far(f).wait_send()
-        for c in range(2):
+    for c in range(2):
+        for f in range(fars):
+            for n in range(4):
+                to_cross(c, f, n).wait_send()
+                if n:
+                    to_near(c, f, n).wait_send()
+                    sum_near(c, f, n).wait_send()
             sum_cross(c, f).wait_send()
-            for n in range(1, 4):
-                sum_near(c, f, n).wait_send()
             if f:
+                to_far(c, f).wait_send()
                 sum_far(c, f).wait_send()
-    own_store.wait()
-    pltpu.make_async_copy(dq, dq, st_sem.at[1]).wait()
-    out.wait()
 
 
 def deliver(*refs):
@@ -345,9 +367,9 @@
     out_shape = tuple(jax.ShapeDtypeStruct(a.shape, BF16) for a in (q_ans, kv_ans, q_prompt, kv_prompt))
     results = pl.pallas_call(
         functools.partial(kernel, nz),
-        out_shape=out_shape,
+        out_shape=tuple(vm(a.shape, BF16) for a in (q_ans, kv_ans, q_prompt, kv_prompt)),
         in_specs=[smem, smem] + [any_spec] * 6,
-        out_specs=(any_spec,) * 4,
+        out_specs=(pl.BlockSpec(memory_space=vm),) * 4,
         scratch_shapes=[
             vm((n_keys // PIECE, 2, PIECE, HD), BF16),
             vm((HD, n_keys), BF16),
@@ -356,29 +378,26 @@
             vm((n_keys, ROWS), F32),
             vm((n_keys, ROWS), F32),
             vm((n_keys, ROWS), BF16),
-            vm((256, ROWS), BF16),
             vm((8, ROWS), F32),
             vm((8, ROWS), F32),
             vm((groups, 8, ROWS), F32),
             vm((groups, 8, ROWS), F32),
             vm((8, ROWS), F32),
             vm((2, n_keys, HD), F32),
-            vm((ROWS, HD), BF16),
-            vm((2, ALEN, HD), BF16),
-            vm((2, PIECE, HD), BF16),
             vm((2, fars, 256, HD), BF16), vm((2, fars, 256, HD), BF16),
             vm((2, fars, 3, PIECE, HD), BF16), vm((2, fars, 3, PIECE, HD), BF16),
             vm((2, fars - 1, PIECE, HD), BF16), vm((2, fars - 1, PIECE, HD), BF16),
-            dma((5,)), dma((3,)),
-            dma((fars,)), dma((fars,)), dma((fars, 4)), dma((fars, 4)), dma((fars, 4)), dma((fars, 4)),
+            dma((5,)),
+            dma((2, fars)), dma((2, fars)), dma((2, fars, 4)), dma((2, fars, 4)), dma((2, fars, 4)), dma((2, fars, 4)),
             dma((2, fars - 1)), dma((2, fars - 1)), dma((2, fars, 3)), dma((2, fars, 3)),
             dma((2, fars)), dma((2, fars)),
         ],
         compiler_params=pltpu.CompilerParams(
             collective_id=0, has_side_effects=True, vmem_limit_bytes=58 * 1024 * 1024),
     )(ans_len, prompt_len, q_ans, kv_ans, q_prompt, kv_prompt, dout_ans, dout_prompt)
+    vm_spec = pl.BlockSpec(memory_space=vm)
     return pl.pallas_call(
-        deliver, out_shape=out_shape, in_specs=[any_spec] * 4, out_specs=(any_spec,) * 4,
+        deliver, out_shape=out_shape, in_specs=[vm_spec] * 4, out_specs=(any_spec,) * 4,
         scratch_shapes=[dma((4,))],
     )(*results)
 

time: 81.9 us -> 69 us (0.84)
  Pallas kernels: 79.9 us -> 64.2 us
  local copies, waits for them, and re-layouts: 0 us -> 2.56 us
    pallas_call x2, Pallas kernels: 79.9 us -> 64.2 us  [the longest x1 62.4 us: per_device(): pl.pallas_call(functools.partial(kernel, nz), out_shape=tuple((vm(a.shape...]
    unnamed x0 -> x8, local copies, waits for them, and re-layouts: none -> 2.56 us
where the time goes in v5:
time: 69 us; the launch traced here: 68.7 us
  Pallas kernels  64.2 us (93%)
  local copies, waits for them, and re-layouts  2.56 us (4%)
  between operations  1.94 us (3%)
    pallas_call x1, Pallas kernels, per_device(): pl.pallas_call(functools.partial(kernel, nz), out_shape=tuple((vm(a.shape...  62.4 us
    unnamed x8, local copies, waits for them, and re-layouts  2.56 us
    pallas_call x1, Pallas kernels, per_device(): pl.pallas_call(deliver, out_shape=out_shape, in_specs=[vm_spec] * 4, out_...  1.82 us

profile of v5, /device:TPU:24, one launch (start us, length us, event | category | flops | bytes accessed | tf_op | source)
XLA Modules:
  0.0 68.7 jit_solution(7076855784416903487)
XLA Ops:
  1.9 62.4 %shard_map.111 = (bf16[128,1024]{1,0:T(8,128)(2,1)S(1)}, bf16[2,128,128]{2,1,0:T(8,128)(2,1)S(1)}, bf16[64,1024]{1,0:T(8,128)(2,1)S(1)}, bf16[2,64,128]{2,1,0:T(8,128)(2,1)S(1)}) custom-call(s32[1]{0:T(128)S(6)} %copy.12.ans_len, s32[1]{0:T(128)S(6)} %copy.13.prompt_len, bf16[128,1024]{1,0:T(8,128)(2,1)} %q_a.1, bf16[2,128,128]{2,1,0:T(8,128)(2,1)} %kv_a.1, ...), custom_call_target="tpu_custom_call" | custom-call | tf_op jit(solution)/shard_map/pallas_call | solution.py:368
  64.3 0.0 copy-start
  64.4 0.7 copy-done
  65.0 0.0 copy-start.1
  65.0 0.6 copy-done.1
  65.7 0.0 copy-start.2
  65.7 0.6 copy-done.2
  66.3 0.0 copy-start.3
  66.3 0.6 copy-done.3
  66.9 1.8 %shard_map.112 = (bf16[128,1024]{1,0:T(8,128)(2,1)}, bf16[2,128,128]{2,1,0:T(8,128)(2,1)}, bf16[64,1024]{1,0:T(8,128)(2,1)}, bf16[2,64,128]{2,1,0:T(8,128)(2,1)}) custom-call(bf16[128,1024]{1,0:T(8,128)(2,1)} %copy-done, bf16[2,128,128]{2,1,0:T(8,128)(2,1)} %copy-done.2, bf16[64,1024]{1,0:T(8,128)(2,1)} %copy-done.1, bf16[2,64,128]{2,1,0:T(8,128)(2,1)} %copy-done.3), custom_call_target="tpu_custom_call" | custom-call | tf_op jit(solution)/shard_map/pallas_call | solution.py:399
Async XLA Ops:
  64.3 0.7 %copy-start = (bf16[128,1024]{1,0:T(8,128)(2,1)}, bf16[128,1024]{1,0:T(8,128)(2,1)S(1)}, u32[]{:S(2)}) copy-start(bf16[128,1024]{1,0:T(8,128)(2,1)S(1)} %get-tuple-element.8.refs_0_) | copy-start | bytes 786436
  65.0 0.6 copy-start.1
  65.7 0.6 copy-start.2
  66.3 0.6 copy-start.3

commit v6 on v5

--- a/solution.py
+++ b/solution.py
@@ -25,17 +25,24 @@
 NT = (((1,), (1,)), ((), ()))
 
 
-NEAR = (0, 1, -1, 2)
+def far_step(f):
+    return 4 * f + f % 2
+
+
+def near_step(f, n):
+    return (0, 1, -1, 2 - 4 * (f % 2))[n]
 
 
 def kernel(nz, ans_len, prompt_len, q_a, kv_a, q_p, kv_p, g_a, g_p,
            dq_a, dkv_a, dq_p, dkv_p,
            kv, kt, q, g, e, dp, ds, mrun, tot, mgrp, rgrp, delta, terms,
+           dq, own_out, prm_out,
            x_out, x_in, near_out, near_in, far_out, far_in,
-           ld_sem, gf_send, gf_recv, gn_send, gn_recv, gx_send, gx_recv,
+           ld_sem, st_sem, gf_send, gf_recv, gn_send, gn_recv, gx_send, gx_recv,
            sf_send, sf_recv, sn_send, sn_recv, sx_send, sx_recv):
     fars = nz // 4
     last = 2 * fars
+    early = fars // 2
     n_keys = 256 * last + 128
     alen = ans_len[0]
     plen = prompt_len[0]
@@ -46,13 +53,16 @@
     cross = {"ans": (1 - par) * nz + z}
 
     def along(step):
-        return (z + side * step + 2 * nz) % nz
+        return (z + side * step + 4 * nz) % nz
 
     def peer(step):
         return {"ans": par * nz + along(step)}
 
     barrier = pltpu.get_barrier_semaphore()
-    steps = sorted({n % nz for n in (1, -1, 2, -2)} | {4 * f for f in range(1, fars)})
+    steps = {n % nz for n in (1, -1, 2, -2)}
+    for f in range(1, fars):
+        steps |= {far_step(f) % nz, -far_step(f) % nz}
+    steps = sorted(steps)
     for other in [peer(step) for step in steps] + [cross]:
         pl.semaphore_signal(barrier, inc=1, device_id=other, device_id_type=MESH)
 
@@ -77,27 +87,46 @@
             device_id=device, device_id_type=MESH)
 
     def to_far(c, f):
-        return remote(kv_p.at[c], kv.at[8 * f, c], gf_send.at[c, f], gf_recv.at[c, f], peer(4 * f))
-
-    def to_near(c, f, n, src=None):
-        return remote(kv.at[8 * f, c] if src is None else src, kv.at[8 * f + n, c],
-                      gn_send.at[c, f, n], gn_recv.at[c, f, n], peer(NEAR[n]))
+        return remote(kv_p.at[c], kv.at[8 * f, c], gf_send.at[c, f], gf_recv.at[c, f], peer(far_step(f)))
+
+    def to_near(c, f, k, n, src=None):
+        return remote(kv.at[8 * f + 4 * k, c] if src is None else src, kv.at[8 * f + 4 * k + n, c],
+                      gn_send.at[c, f, k, n], gn_recv.at[c, f, k, n], peer(near_step(f, n)))
 
     def to_cross(c, f, n, src=None):
         return remote(kv.at[8 * f + n, c] if src is None else src, kv.at[8 * f + 4 + n, c],
                       gx_send.at[c, f, n], gx_recv.at[c, f, n], cross)
 
     def spread_own(c):
+        to_cross(c, 0, 0, kv_p.at[c]).start()
         for n in range(1, 4):
-            to_near(c, 0, n, kv_p.at[c]).start()
-        to_cross(c, 0, 0, kv_p.at[c]).start()
+            to_near(c, 0, 0, n, kv_p.at[c]).start()
 
     def spread_far(c):
         for f in range(1, fars):
             to_far(c, f).wait_recv()
+            to_cross(c, f, 0).start()
             for n in range(1, 4):
-                to_near(c, f, n).start()
-            to_cross(c, f, 0).start()
+                to_near(c, f, 0, n).start()
+
+    def spread_cross(c):
+        for f in range(early):
+            to_cross(c, f, 0).wait_recv()
+            for n in range(1, 4):
+                to_near(c, f, 1, n).start()
+
+    def near_arrived(c, f, k):
+        for n in range(1, 4):
+            to_near(c, f, k, n).wait_recv()
+
+    def near_to_cross(c, f):
+        for n in range(1, 4):
+            to_near(c, f, 0, n).wait_recv()
+            to_cross(c, f, n).start()
+
+    def cross_arrived(c, f):
+        for n in range(4):
+            to_cross(c, f, n).wait_recv()
 
     K, V = 0, 1
     for f in range(1, fars):
@@ -160,36 +189,28 @@
 
     def bases(f, k):
         half = par if k == 0 else 1 - par
-        return [(half * nz + along(-(NEAR[n] + 4 * f))) * PIECE for n in range(4)]
+        return [(half * nz + along(-(near_step(f, n) + far_step(f)))) * PIECE for n in range(4)]
+
+    def loop(first, stop, *steps):
+        def body(i, carry):
+            f = first + i if stop >= first else first - 1 - i
+            for step in steps:
+                step(f)
+            return carry
+        lax.fori_loop(0, abs(stop - first), body, 0)
 
     score_group(last, [], True)
     spread_far(K)
-
-    def this_half(f, carry):
-        for n in range(1, 4):
-            to_near(K, f, n).wait_recv()
-            to_cross(K, f, n).start()
-        score_group(2 * f, bases(f, 0))
-        return carry
-
-    def other_half(f, carry):
-        for n in range(4):
-            to_cross(K, f, n).wait_recv()
-        score_group(2 * f + 1, bases(f, 1))
-        return carry
-
-    lax.fori_loop(0, fars, this_half, 0)
+    spread_cross(K)
+    loop(0, early, lambda f: near_arrived(K, f, 0), lambda f: score_group(2 * f, bases(f, 0)))
+    loop(early, fars, lambda f: near_to_cross(K, f), lambda f: score_group(2 * f, bases(f, 0)))
     spread_own(V)
     spread_far(V)
-    lax.fori_loop(0, fars, other_half, 0)
-
-    def values_on(f, carry):
-        for n in range(1, 4):
-            to_near(V, f, n).wait_recv()
-            to_cross(V, f, n).start()
-        return carry
-
-    lax.fori_loop(0, fars, values_on, 0)
+    spread_cross(V)
+    loop(0, early, lambda f: near_arrived(K, f, 1), lambda f: score_group(2 * f + 1, bases(f, 1)))
+    loop(early, fars, lambda f: cross_arrived(K, f), lambda f: score_group(2 * f + 1, bases(f, 1)))
+    for f in range(early, fars):
+        near_to_cross(V, f)
 
     m8 = mrun[...]
     top = jnp.max(m8, axis=0, keepdims=True)
@@ -228,43 +249,52 @@
 
     def query_terms(j):
         lanes = slice(j * LANES, (j + 1) * LANES)
-        rows = jnp.dot(kt[...], ds[:, lanes], preferred_element_type=F32).T.astype(BF16)
-        out, tokens, first = (dq_a, ALEN, j * LANES) if j * LANES < A_ROWS else (dq_p, PIECE, j * LANES - A_ROWS)
-        for i in range(LANES // tokens):
-            head = first // tokens + i
-            out[:, head * HD:(head + 1) * HD] = rows[i * tokens:(i + 1) * tokens]
+        rows = jnp.dot(kt[...], ds[:, lanes], preferred_element_type=F32)
+        dq[lanes, :] = rows.T.astype(BF16)
 
     def sum_cross(c, f):
-        return remote(x_out.at[c, f], x_in.at[c, f], sx_send.at[c, f], sx_recv.at[c, f], cross)
-
-    def sum_near(c, f, n):
-        return remote(near_out.at[c, f, n - 1], near_in.at[c, f, n - 1],
-                      sn_send.at[c, f, n - 1], sn_recv.at[c, f, n - 1], peer(-NEAR[n]))
+        rows = pl.ds(0, 256 if f >= early else PIECE)
+        return remote(x_out.at[c, f, rows], x_in.at[c, f, rows], sx_send.at[c, f], sx_recv.at[c, f], cross)
+
+    def sum_near(c, f, k, n):
+        return remote(near_out.at[c, f, k, n - 1], near_in.at[c, f, k, n - 1],
+                      sn_send.at[c, f, k, n - 1], sn_recv.at[c, f, k, n - 1], peer(-near_step(f, n)))
 
     def sum_far(c, f):
         return remote(far_out.at[c, f - 1], far_in.at[c, f - 1],
-                      sf_send.at[c, f - 1], sf_recv.at[c, f - 1], peer(-4 * f))
-
-    def send_cross(c, f):
-        x_out[c, f] = terms[c, pl.ds(rows_of(2 * f + 1), 256), :].astype(BF16)
-        sum_cross(c, f).start()
-
-    def send_near(c, f):
-        sum_cross(c, f).wait_recv()
-        row = 512 * f
+                      sf_send.at[c, f - 1], sf_recv.at[c, f - 1], peer(-far_step(f)))
+
+    def send_near(c, f, k):
+        if k == 0 and f >= early:
+            sum_cross(c, f).wait_recv()
+        row = 512 * f + 256 * k
         for n in range(1, 4):
             part = terms[c, row + n * PIECE:row + (n + 1) * PIECE, :]
-            part = part + x_in[c, f, n * PIECE:(n + 1) * PIECE, :].astype(F32)
-            near_out[c, f, n - 1] = part.astype(BF16)
-            sum_near(c, f, n).start()
+            if k == 0 and f >= early:
+                part = part + x_in[c, f, n * PIECE:(n + 1) * PIECE, :].astype(F32)
+            near_out[c, f, k, n - 1] = part.astype(BF16)
+            sum_near(c, f, k, n).start()
+
+    def near_sum(c, f, k):
+        row = 512 * f + 256 * k
+        acc = terms[c, row:row + PIECE, :]
+        for n in range(1, 4):
+            sum_near(c, f, k, n).wait_recv()
+            acc = acc + near_in[c, f, k, n - 1].astype(F32)
+        return acc
+
+    def send_cross(c, f):
+        if f >= early:
+            x_out[c, f] = terms[c, 512 * f + 256:512 * f + 512, :].astype(BF16)
+        else:
+            x_out[c, f, 0:PIECE] = near_sum(c, f, 1).astype(BF16)
+        sum_cross(c, f).start()
 
     def held(c, f):
-        row = 512 * f
-        acc = terms[c, row:row + PIECE, :] + x_in[c, f, 0:PIECE, :].astype(F32)
-        for n in range(1, 4):
-            sum_near(c, f, n).wait_recv()
-            acc = acc + near_in[c, f, n - 1].astype(F32)
-        return acc
+        acc = near_sum(c, f, 0)
+        if f < early:
+            sum_cross(c, f).wait_recv()
+        return acc + x_in[c, f, 0:PIECE, :].astype(F32)
 
     def send_far(c, f):
         far_out[c, f - 1] = held(c, f).astype(BF16)
@@ -275,86 +305,93 @@
         for f in range(1, fars):
             sum_far(c, f).wait_recv()
             acc = acc + far_in[c, f - 1].astype(F32)
-        dkv_p[c] = acc.astype(BF16)
-
-    def value_cross(i, carry):
-        f = fars - 1 - i
-        value_terms(2 * f + 1)
+        prm_out[c] = acc.astype(BF16)
+
+    late_groups = list(range(fars - 1, early - 1, -1))
+    early_groups = list(range(early - 1, -1, -1))
+    far_groups = list(range(fars - 1, 0, -1))
+
+    def both_halves(c, fn):
+        for f in late_groups:
+            fn(2 * f + 1)
+            send_cross(c, f)
+        for f in early_groups:
+            fn(2 * f + 1)
+            send_near(c, f, 1)
+        for f in early_groups:
+            fn(2 * f)
+            send_near(c, f, 0)
+        loop(fars, early, lambda f: fn(2 * f))
+        fn(last, 128)
+
+    both_halves(V, value_terms)
+    delta_terms(last, 128)
+    for f in late_groups:
+        send_near(V, f, 0)
+    loop(0, early, lambda f: near_arrived(V, f, 0), lambda f: delta_terms(2 * f))
+    loop(early, fars, lambda f: delta_terms(2 * f))
+    for f in early_groups:
         send_cross(V, f)
-        return carry
-
-    def key_cross(i, carry):
-        f = fars - 1 - i
-        key_terms(2 * f + 1)
-        send_cross(K, f)
-        return carry
-
-    def own_delta(f, carry):
-        delta_terms(2 * f)
-        return carry
-
-    def cross_delta(f, carry):
-        for n in range(4):
-            to_cross(V, f, n).wait_recv()
-        delta_terms(2 * f + 1)
-        return carry
-
-    lax.fori_loop(0, fars, value_cross, 0)
-    value_terms(last, 128)
-    lax.fori_loop(0, fars, lambda i, carry: (value_terms(2 * (fars - 1 - i)), carry)[1], 0)
-    delta_terms(last, 128)
-    lax.fori_loop(0, fars, own_delta, 0)
-    lax.fori_loop(0, fars, cross_delta, 0)
+    loop(0, early, lambda f: near_arrived(V, f, 1), lambda f: delta_terms(2 * f + 1))
+    loop(early, fars, lambda f: cross_arrived(V, f), lambda f: delta_terms(2 * f + 1))
     delta[...] = jnp.broadcast_to(jnp.sum(delta[...], axis=0, keepdims=True), delta.shape)
-    for f in range(fars - 1, fars // 2 - 1, -1):
-        send_near(V, f)
-    lax.fori_loop(0, fars, key_cross, 0)
-    for f in range(fars // 2 - 1, -1, -1):
-        send_near(V, f)
-    lax.fori_loop(0, fars, lambda i, carry: (key_terms(2 * (fars - 1 - i)), carry)[1], 0)
-    key_terms(last, 128)
-    dkv_a[...] = terms[:, 256 * last:256 * last + ALEN, :].astype(BF16)
+    both_halves(K, key_terms)
+    own_out[...] = terms[:, 256 * last:256 * last + ALEN, :].astype(BF16)
+    own_store = pltpu.make_async_copy(own_out, dkv_a, st_sem.at[0])
+    own_store.start()
+    for f in far_groups:
+        send_far(V, f)
     for s in range(n_keys // 128):
         kt[:, s * 128:(s + 1) * 128] = kv[2 * s:2 * s + 2, 0].reshape(128, HD).T
     query_terms(0)
     query_terms(1)
-    todo_near = list(range(fars - 1, -1, -1))
-    todo_far = list(range(fars - 1, 0, -1))
-    for f in todo_far:
-        send_far(V, f)
-    send_near(K, todo_near.pop(0))
+    for f in late_groups:
+        send_near(K, f, 0)
     query_terms(2)
     query_terms(3)
-    send_near(K, todo_near.pop(0))
+    for f in early_groups:
+        send_cross(K, f)
     query_terms(4)
     query_terms(5)
-    for f in todo_near:
-        send_near(K, f)
-    for f in todo_far:
+    for h in range(HEADS):
+        cols = pl.ds(h * HD, HD)
+        pltpu.make_async_copy(dq.at[pl.ds(h * ALEN, ALEN)], dq_a.at[:, cols], st_sem.at[1]).start()
+        pltpu.make_async_copy(dq.at[pl.ds(A_ROWS + h * PIECE, PIECE)], dq_p.at[:, cols], st_sem.at[1]).start()
+    for f in far_groups:
         send_far(K, f)
     finish(V)
     finish(K)
+    prompt_store = pltpu.make_async_copy(prm_out, dkv_p, st_sem.at[2])
+    prompt_store.start()
+
     for c in range(2):
         for f in range(fars):
-            for n in range(4):
+            for n in range(4 if f >= early else 1):
                 to_cross(c, f, n).wait_send()
-                if n:
-                    to_near(c, f, n).wait_send()
-                    sum_near(c, f, n).wait_send()
+            for k in range(1 if f >= early else 2):
+                for n in range(1, 4):
+                    to_near(c, f, k, n).wait_send()
+                    sum_near(c, f, k, n).wait_send()
             sum_cross(c, f).wait_send()
             if f:
                 to_far(c, f).wait_send()
                 sum_far(c, f).wait_send()
+    own_store.wait()
+    pltpu.make_async_copy(dq, dq, st_sem.at[1]).wait()
+    prompt_store.wait()
 
 
 def deliver(*refs):
-    sems = refs[-1]
-    count = len(refs) // 2
-    copies = [pltpu.make_async_copy(refs[i], refs[count + i], sems.at[i]) for i in range(count)]
-    for copy in copies:
-        copy.start()
-    for copy in copies:
-        copy.wait()
+    count = len(refs) // 3
+    loads, stores = refs[-2:]
+    ins, outs, held = refs[:count], refs[count:2 * count], refs[2 * count:3 * count]
+    for i in range(count):
+        pltpu.make_async_copy(ins[i], held[i], loads.at[i]).start()
+    for i in range(count):
+        pltpu.make_async_copy(ins[i], held[i], loads.at[i]).wait()
+        pltpu.make_async_copy(held[i], outs[i], stores.at[i]).start()
+    for i in range(count):
+        pltpu.make_async_copy(held[i], outs[i], stores.at[i]).wait()
 
 
 def per_device(nz, q_ans, kv_ans, q_prompt, kv_prompt, dout_ans, dout_prompt, ans_len, prompt_len):
@@ -367,9 +404,9 @@
     out_shape = tuple(jax.ShapeDtypeStruct(a.shape, BF16) for a in (q_ans, kv_ans, q_prompt, kv_prompt))
     results = pl.pallas_call(
         functools.partial(kernel, nz),
-        out_shape=tuple(vm(a.shape, BF16) for a in (q_ans, kv_ans, q_prompt, kv_prompt)),
+        out_shape=out_shape,
         in_specs=[smem, smem] + [any_spec] * 6,
-        out_specs=(pl.BlockSpec(memory_space=vm),) * 4,
+        out_specs=(any_spec,) * 4,
         scratch_shapes=[
             vm((n_keys // PIECE, 2, PIECE, HD), BF16),
             vm((HD, n_keys), BF16),
@@ -384,21 +421,24 @@
             vm((groups, 8, ROWS), F32),
             vm((8, ROWS), F32),
             vm((2, n_keys, HD), F32),
+            vm((ROWS, HD), BF16),
+            vm((2, ALEN, HD), BF16),
+            vm((2, PIECE, HD), BF16),
             vm((2, fars, 256, HD), BF16), vm((2, fars, 256, HD), BF16),
-            vm((2, fars, 3, PIECE, HD), BF16), vm((2, fars, 3, PIECE, HD), BF16),
+            vm((2, fars, 2, 3, PIECE, HD), BF16), vm((2, fars, 2, 3, PIECE, HD), BF16),
             vm((2, fars - 1, PIECE, HD), BF16), vm((2, fars - 1, PIECE, HD), BF16),
-            dma((5,)),
-            dma((2, fars)), dma((2, fars)), dma((2, fars, 4)), dma((2, fars, 4)), dma((2, fars, 4)), dma((2, fars, 4)),
-            dma((2, fars - 1)), dma((2, fars - 1)), dma((2, fars, 3)), dma((2, fars, 3)),
+            dma((5,)), dma((3,)),
+            dma((2, fars)), dma((2, fars)), dma((2, fars, 2, 4)), dma((2, fars, 2, 4)),
+            dma((2, fars, 4)), dma((2, fars, 4)),
+            dma((2, fars - 1)), dma((2, fars - 1)), dma((2, fars, 2, 3)), dma((2, fars, 2, 3)),
             dma((2, fars)), dma((2, fars)),
         ],
         compiler_params=pltpu.CompilerParams(
             collective_id=0, has_side_effects=True, vmem_limit_bytes=58 * 1024 * 1024),
     )(ans_len, prompt_len, q_ans, kv_ans, q_prompt, kv_prompt, dout_ans, dout_prompt)
-    vm_spec = pl.BlockSpec(memory_space=vm)
     return pl.pallas_call(
-        deliver, out_shape=out_shape, in_specs=[vm_spec] * 4, out_specs=(any_spec,) * 4,
-        scratch_shapes=[dma((4,))],
+        deliver, out_shape=out_shape, in_specs=[any_spec] * 4, out_specs=(any_spec,) * 4,
+        scratch_shapes=[vm(a.shape, BF16) for a in out_shape] + [dma((4,)), dma((4,))],
     )(*results)
 
 

time: 69 us -> 66.4 us (0.962)
  local copies, waits for them, and re-layouts: 2.56 us -> 0 us
    unnamed x8 -> x0, local copies, waits for them, and re-layouts: 2.56 us -> none
where the time goes in v6:
time: 66.4 us; the launch traced here: 66.3 us
  Pallas kernels  64.3 us (97%)
  between operations  1.93 us (3%)
    pallas_call x1, Pallas kernels, per_device(): pl.pallas_call(functools.partial(kernel, nz), out_shape=out_shape, in_spe...  62.6 us
    pallas_call x1, Pallas kernels, per_device(): pl.pallas_call(deliver, out_shape=out_shape, in_specs=[any_spec] * 4, out...  1.79 us

profile of v6, /device:TPU:24, one launch (start us, length us, event | category | flops | bytes accessed | tf_op | source)
XLA Modules:
  0.0 66.3 jit_solution(17273020813526488827)
XLA Ops:
  1.9 62.6 %shard_map.111 = (bf16[128,1024]{1,0:T(8,128)(2,1)}, bf16[2,128,128]{2,1,0:T(8,128)(2,1)}, bf16[64,1024]{1,0:T(8,128)(2,1)}, bf16[2,64,128]{2,1,0:T(8,128)(2,1)}) custom-call(s32[1]{0:T(128)S(6)} %copy.12.ans_len, s32[1]{0:T(128)S(6)} %copy.13.prompt_len, bf16[128,1024]{1,0:T(8,128)(2,1)} %q_a.1, bf16[2,128,128]{2,1,0:T(8,128)(2,1)} %kv_a.1, ...), custom_call_target="tpu_custom_call" | custom-call | tf_op jit(solution)/shard_map/pallas_call | solution.py:405
  64.5 1.8 %shard_map.112 = (bf16[128,1024]{1,0:T(8,128)(2,1)}, bf16[2,128,128]{2,1,0:T(8,128)(2,1)}, bf16[64,1024]{1,0:T(8,128)(2,1)}, bf16[2,64,128]{2,1,0:T(8,128)(2,1)}) custom-call(bf16[128,1024]{1,0:T(8,128)(2,1)} %get-tuple-element.8.refs_0_, bf16[2,128,128]{2,1,0:T(8,128)(2,1)} %get-tuple-element.9.refs_1_, bf16[64,1024]{1,0:T(8,128)(2,1)} %get-tuple-element.10.refs_2_, ...), custom_call_target="tpu_custom_call" | custom-call | tf_op jit(solution)/shard_map/pallas_call | solution.py:439

commit v7 on v6

--- a/solution.py
+++ b/solution.py
@@ -35,7 +35,7 @@
 
 def kernel(nz, ans_len, prompt_len, q_a, kv_a, q_p, kv_p, g_a, g_p,
            dq_a, dkv_a, dq_p, dkv_p,
-           kv, kt, q, g, e, dp, ds, mrun, tot, mgrp, rgrp, delta, terms,
+           kv, kt, q, g, e, dp, ds, pbuf, mrun, tot, mgrp, rgrp, delta, terms,
            dq, own_out, prm_out,
            x_out, x_in, near_out, near_in, far_out, far_in,
            ld_sem, st_sem, gf_send, gf_recv, gn_send, gn_recv, gx_send, gx_recv,
@@ -53,10 +53,12 @@
     cross = {"ans": (1 - par) * nz + z}
 
     def along(step):
-        return (z + side * step + 4 * nz) % nz
+        return (z + side * step + 4 * nz) & (nz - 1)
+
+    places = {step: par * nz + along(step) for step in range(nz)}
 
     def peer(step):
-        return {"ans": par * nz + along(step)}
+        return {"ans": places[step % nz] if isinstance(step, int) else par * nz + along(step)}
 
     barrier = pltpu.get_barrier_semaphore()
     steps = {n % nz for n in (1, -1, 2, -2)}
@@ -86,54 +88,41 @@
             src_ref=src, dst_ref=dst, send_sem=send, recv_sem=recv,
             device_id=device, device_id_type=MESH)
 
-    def to_far(c, f):
-        return remote(kv_p.at[c], kv.at[8 * f, c], gf_send.at[c, f], gf_recv.at[c, f], peer(far_step(f)))
-
-    def to_near(c, f, k, n, src=None):
-        return remote(kv.at[8 * f + 4 * k, c] if src is None else src, kv.at[8 * f + 4 * k + n, c],
-                      gn_send.at[c, f, k, n], gn_recv.at[c, f, k, n], peer(near_step(f, n)))
-
-    def to_cross(c, f, n, src=None):
-        return remote(kv.at[8 * f + n, c] if src is None else src, kv.at[8 * f + 4 + n, c],
-                      gx_send.at[c, f, n], gx_recv.at[c, f, n], cross)
-
-    def spread_own(c):
-        to_cross(c, 0, 0, kv_p.at[c]).start()
-        for n in range(1, 4):
-            to_near(c, 0, 0, n, kv_p.at[c]).start()
-
-    def spread_far(c):
-        for f in range(1, fars):
-            to_far(c, f).wait_recv()
-            to_cross(c, f, 0).start()
-            for n in range(1, 4):
-                to_near(c, f, 0, n).start()
-
-    def spread_cross(c):
-        for f in range(early):
-            to_cross(c, f, 0).wait_recv()
-            for n in range(1, 4):
-                to_near(c, f, 1, n).start()
-
-    def near_arrived(c, f, k):
-        for n in range(1, 4):
-            to_near(c, f, k, n).wait_recv()
-
-    def near_to_cross(c, f):
-        for n in range(1, 4):
-            to_near(c, f, 0, n).wait_recv()
-            to_cross(c, f, n).start()
-
-    def cross_arrived(c, f):
+    def to_far(f):
+        return remote(kv_p, kv.at[8 * f], gf_send.at[f], gf_recv.at[f], peer(far_step(f)))
+
+    def to_near(f, k, n, src=None):
+        return remote(kv.at[8 * f + 4 * k] if src is None else src, kv.at[8 * f + 4 * k + n],
+                      gn_send.at[f, k, n], gn_recv.at[f, k, n], peer(near_step(f, n)))
+
+    def to_cross(f, n, src=None):
+        return remote(kv.at[8 * f + n] if src is None else src, kv.at[8 * f + 4 + n],
+                      gx_send.at[f, n], gx_recv.at[f, n], cross)
+
+    def spread_cross(f):
+        to_cross(f, 0).wait_recv()
+        for n in range(1, 4):
+            to_near(f, 1, n).start()
+
+    def near_arrived(f, k):
+        for n in range(1, 4):
+            to_near(f, k, n).wait_recv()
+
+    def near_to_cross(f):
+        for n in range(1, 4):
+            to_near(f, 0, n).wait_recv()
+            to_cross(f, n).start()
+
+    def cross_arrived(f):
         for n in range(4):
-            to_cross(c, f, n).wait_recv()
+            to_cross(f, n).wait_recv()
 
     K, V = 0, 1
     for f in range(1, fars):
-        to_far(K, f).start()
-    spread_own(K)
-    for f in range(1, fars):
-        to_far(V, f).start()
+        to_far(f).start()
+    to_cross(0, 0, kv_p).start()
+    for n in range(1, 4):
+        to_near(0, 0, n, kv_p).start()
 
     pltpu.make_async_copy(q, q, ld_sem.at[0]).wait()
     pltpu.make_async_copy(g, g, ld_sem.at[1]).wait()
@@ -159,6 +148,7 @@
         rows = pl.ds(rows_of(s), n)
         slots = pl.ds(4 * s, n // PIECE)
         keys = kv[slots, 0].reshape(n, HD)
+        values = kv[slots, 1].reshape(n, HD)
         for j in range(CHUNKS):
             lanes = slice(j * LANES, (j + 1) * LANES)
             lim, lim_own = limits(j)
@@ -186,6 +176,7 @@
             mrun[:, lanes] = new
             mgrp[s, :, lanes] = new
             e[rows, lanes] = ex.reshape(n, LANES)
+            dp[rows, lanes] = lax.dot_general(values, g[lanes, :], NT, preferred_element_type=F32)
 
     def bases(f, k):
         half = par if k == 0 else 1 - par
@@ -199,18 +190,32 @@
             return carry
         lax.fori_loop(0, abs(stop - first), body, 0)
 
+    def loop(first, stop, *steps):
+        def body(i, carry):
+            f = first + i if stop >= first else first - 1 - i
+            for step in steps:
+                step(f)
+            return carry
+        lax.fori_loop(0, abs(stop - first), body, 0)
+
+    def score(f, k):
+        score_group(2 * f + k, bases(f, k))
+
     score_group(last, [], True)
-    spread_far(K)
-    spread_cross(K)
-    loop(0, early, lambda f: near_arrived(K, f, 0), lambda f: score_group(2 * f, bases(f, 0)))
-    loop(early, fars, lambda f: near_to_cross(K, f), lambda f: score_group(2 * f, bases(f, 0)))
-    spread_own(V)
-    spread_far(V)
-    spread_cross(V)
-    loop(0, early, lambda f: near_arrived(K, f, 1), lambda f: score_group(2 * f + 1, bases(f, 1)))
-    loop(early, fars, lambda f: cross_arrived(K, f), lambda f: score_group(2 * f + 1, bases(f, 1)))
+    for f in range(1, fars):
+        to_far(f).wait_recv()
+        to_cross(f, 0).start()
+        for n in range(1, 4):
+            to_near(f, 0, n).start()
+    for f in range(early):
+        spread_cross(f)
+        near_arrived(f, 0)
+        score(f, 0)
     for f in range(early, fars):
-        near_to_cross(V, f)
+        near_to_cross(f)
+    loop(early, fars, lambda f: score(f, 0))
+    loop(0, early, lambda f: near_arrived(f, 1), lambda f: score(f, 1))
+    loop(early, fars, lambda f: cross_arrived(f), lambda f: score(f, 1))
 
     m8 = mrun[...]
     top = jnp.max(m8, axis=0, keepdims=True)
@@ -225,18 +230,11 @@
         for j in range(CHUNKS):
             lanes = slice(j * LANES, (j + 1) * LANES)
             p = e[rows, lanes].reshape(n // 8, 8, LANES) * rgrp[s, :, lanes][None]
-            ds[rows, lanes] = p.reshape(n, LANES).astype(BF16)
-        terms[1, rows, :] = jnp.dot(ds[rows, :], g[...], preferred_element_type=F32)
-
-    def delta_terms(s, n=256):
-        rows = pl.ds(rows_of(s), n)
-        values = kv[pl.ds(4 * s, n // PIECE), 1].reshape(n, HD)
-        for j in range(CHUNKS):
-            lanes = slice(j * LANES, (j + 1) * LANES)
-            dprob = lax.dot_general(values, g[lanes, :], NT, preferred_element_type=F32)
-            dp[rows, lanes] = dprob
-            prod = ds[rows, lanes].astype(F32) * dprob
+            pb = p.reshape(n, LANES).astype(BF16)
+            pbuf[0:n, lanes] = pb
+            prod = pb.astype(F32) * dp[rows, lanes]
             delta[:, lanes] += jnp.sum(prod.reshape(n // 8, 8, LANES), axis=0)
+        terms[1, rows, :] = jnp.dot(pbuf[0:n], g[...], preferred_element_type=F32)
 
     def key_terms(s, n=256):
         rows = pl.ds(rows_of(s), n)
@@ -311,73 +309,84 @@
     early_groups = list(range(early - 1, -1, -1))
     far_groups = list(range(fars - 1, 0, -1))
 
-    def both_halves(c, fn):
-        for f in late_groups:
-            fn(2 * f + 1)
-            send_cross(c, f)
-        for f in early_groups:
-            fn(2 * f + 1)
-            send_near(c, f, 1)
-        for f in early_groups:
-            fn(2 * f)
-            send_near(c, f, 0)
-        loop(fars, early, lambda f: fn(2 * f))
-        fn(last, 128)
-
-    both_halves(V, value_terms)
-    delta_terms(last, 128)
+    for f in late_groups:
+        value_terms(2 * f + 1)
+        send_cross(V, f)
+    for f in early_groups:
+        value_terms(2 * f + 1)
+        send_near(V, f, 1)
+    for f in early_groups:
+        value_terms(2 * f)
+        send_near(V, f, 0)
+    loop(fars, early, lambda f: value_terms(2 * f))
+    value_terms(last, 128)
+    delta[...] = jnp.broadcast_to(jnp.sum(delta[...], axis=0, keepdims=True), delta.shape)
+    for f in late_groups:
+        key_terms(2 * f + 1)
+        send_cross(K, f)
     for f in late_groups:
         send_near(V, f, 0)
-    loop(0, early, lambda f: near_arrived(V, f, 0), lambda f: delta_terms(2 * f))
-    loop(early, fars, lambda f: delta_terms(2 * f))
+    for f in early_groups:
+        key_terms(2 * f + 1)
+        send_near(K, f, 1)
     for f in early_groups:
         send_cross(V, f)
-    loop(0, early, lambda f: near_arrived(V, f, 1), lambda f: delta_terms(2 * f + 1))
-    loop(early, fars, lambda f: cross_arrived(V, f), lambda f: delta_terms(2 * f + 1))
-    delta[...] = jnp.broadcast_to(jnp.sum(delta[...], axis=0, keepdims=True), delta.shape)
-    both_halves(K, key_terms)
+    for f in early_groups:
+        key_terms(2 * f)
+        send_near(K, f, 0)
+    loop(fars, early, lambda f: key_terms(2 * f))
+    for f in late_groups:
+        send_near(K, f, 0)
+    key_terms(last, 128)
     own_out[...] = terms[:, 256 * last:256 * last + ALEN, :].astype(BF16)
     own_store = pltpu.make_async_copy(own_out, dkv_a, st_sem.at[0])
     own_store.start()
     for f in far_groups:
         send_far(V, f)
+    for f in early_groups:
+        send_cross(K, f)
     for s in range(n_keys // 128):
         kt[:, s * 128:(s + 1) * 128] = kv[2 * s:2 * s + 2, 0].reshape(128, HD).T
-    query_terms(0)
-    query_terms(1)
-    for f in late_groups:
-        send_near(K, f, 0)
-    query_terms(2)
-    query_terms(3)
-    for f in early_groups:
-        send_cross(K, f)
-    query_terms(4)
-    query_terms(5)
+    for j in range(CHUNKS // 2):
+        query_terms(j)
+    late_far = [f for f in far_groups if f >= early]
+    for f in late_far:
+        send_far(K, f)
+    for j in range(CHUNKS // 2, CHUNKS):
+        query_terms(j)
+    for f in far_groups:
+        if f not in late_far:
+            send_far(K, f)
     for h in range(HEADS):
         cols = pl.ds(h * HD, HD)
         pltpu.make_async_copy(dq.at[pl.ds(h * ALEN, ALEN)], dq_a.at[:, cols], st_sem.at[1]).start()
         pltpu.make_async_copy(dq.at[pl.ds(A_ROWS + h * PIECE, PIECE)], dq_p.at[:, cols], st_sem.at[1]).start()
-    for f in far_groups:
-        send_far(K, f)
+
+    def sent(c):
+        for f in range(fars):
+            for k in range(1 if f >= early else 2):
+                for n in range(1, 4):
+                    sum_near(c, f, k, n).wait_send()
+            sum_cross(c, f).wait_send()
+            if f:
+                sum_far(c, f).wait_send()
+
     finish(V)
+    for f in range(fars):
+        for n in range(4 if f >= early else 1):
+            to_cross(f, n).wait_send()
+        for k in range(1 if f >= early else 2):
+            for n in range(1, 4):
+                to_near(f, k, n).wait_send()
+        if f:
+            to_far(f).wait_send()
+    sent(V)
+    own_store.wait()
+    pltpu.make_async_copy(dq, dq, st_sem.at[1]).wait()
     finish(K)
     prompt_store = pltpu.make_async_copy(prm_out, dkv_p, st_sem.at[2])
     prompt_store.start()
-
-    for c in range(2):
-        for f in range(fars):
-            for n in range(4 if f >= early else 1):
-                to_cross(c, f, n).wait_send()
-            for k in range(1 if f >= early else 2):
-                for n in range(1, 4):
-                    to_near(c, f, k, n).wait_send()
-                    sum_near(c, f, k, n).wait_send()
-            sum_cross(c, f).wait_send()
-            if f:
-                to_far(c, f).wait_send()
-                sum_far(c, f).wait_send()
-    own_store.wait()
-    pltpu.make_async_copy(dq, dq, st_sem.at[1]).wait()
+    sent(K)
     prompt_store.wait()
 
 
@@ -415,6 +424,7 @@
             vm((n_keys, ROWS), F32),
             vm((n_keys, ROWS), F32),
             vm((n_keys, ROWS), BF16),
+            vm((256, ROWS), BF16),
             vm((8, ROWS), F32),
             vm((8, ROWS), F32),
             vm((groups, 8, ROWS), F32),
@@ -428,8 +438,8 @@
             vm((2, fars, 2, 3, PIECE, HD), BF16), vm((2, fars, 2, 3, PIECE, HD), BF16),
             vm((2, fars - 1, PIECE, HD), BF16), vm((2, fars - 1, PIECE, HD), BF16),
             dma((5,)), dma((3,)),
-            dma((2, fars)), dma((2, fars)), dma((2, fars, 2, 4)), dma((2, fars, 2, 4)),
-            dma((2, fars, 4)), dma((2, fars, 4)),
+            dma((fars,)), dma((fars,)), dma((fars, 2, 4)), dma((fars, 2, 4)),
+            dma((fars, 4)), dma((fars, 4)),
             dma((2, fars - 1)), dma((2, fars - 1)), dma((2, fars, 2, 3)), dma((2, fars, 2, 3)),
             dma((2, fars)), dma((2, fars)),
         ],

time: 66.4 us -> 63 us (0.949)
  Pallas kernels: 64.3 us -> 60.9 us
    pallas_call x1, Pallas kernels: 62.6 us -> 59.1 us  [per_device(): pl.pallas_call(functools.partial(kernel, nz), out_shape=out_shape, in_spe...]
where the time goes in v7:
time: 63 us; the launch traced here: 62.8 us
  Pallas kernels  60.9 us (97%)
  between operations  1.93 us (3%)
    pallas_call x1, Pallas kernels, per_device(): pl.pallas_call(functools.partial(kernel, nz), out_shape=out_shape, in_spe...  59.1 us
    pallas_call x1, Pallas kernels, per_device(): pl.pallas_call(deliver, out_shape=out_shape, in_specs=[any_spec] * 4, out...  1.79 us

profile of v7, /device:TPU:24, one launch (start us, length us, event | category | flops | bytes accessed | tf_op | source)
XLA Modules:
  0.0 62.8 jit_solution(3753208038443158644)
XLA Ops:
  1.9 59.1 %shard_map.111 = (bf16[128,1024]{1,0:T(8,128)(2,1)}, bf16[2,128,128]{2,1,0:T(8,128)(2,1)}, bf16[64,1024]{1,0:T(8,128)(2,1)}, bf16[2,64,128]{2,1,0:T(8,128)(2,1)}) custom-call(s32[1]{0:T(128)S(6)} %copy.12.ans_len, s32[1]{0:T(128)S(6)} %copy.13.prompt_len, bf16[128,1024]{1,0:T(8,128)(2,1)} %q_a.1, bf16[2,128,128]{2,1,0:T(8,128)(2,1)} %kv_a.1, ...), custom_call_target="tpu_custom_call" | custom-call | tf_op jit(solution)/shard_map/pallas_call | solution.py:414
  61.0 1.8 %shard_map.112 = (bf16[128,1024]{1,0:T(8,128)(2,1)}, bf16[2,128,128]{2,1,0:T(8,128)(2,1)}, bf16[64,1024]{1,0:T(8,128)(2,1)}, bf16[2,64,128]{2,1,0:T(8,128)(2,1)}) custom-call(bf16[128,1024]{1,0:T(8,128)(2,1)} %get-tuple-element.8.refs_0_, bf16[2,128,128]{2,1,0:T(8,128)(2,1)} %get-tuple-element.9.refs_1_, bf16[64,1024]{1,0:T(8,128)(2,1)} %get-tuple-element.10.refs_2_, ...), custom_call_target="tpu_custom_call" | custom-call | tf_op jit(solution)/shard_map/pallas_call | solution.py:449

commit v8 on v7

--- a/solution.py
+++ b/solution.py
@@ -37,12 +37,10 @@
            dq_a, dkv_a, dq_p, dkv_p,
            kv, kt, q, g, e, dp, ds, pbuf, mrun, tot, mgrp, rgrp, delta, terms,
            dq, own_out, prm_out,
-           x_out, x_in, near_out, near_in, far_out, far_in,
-           ld_sem, st_sem, gf_send, gf_recv, gn_send, gn_recv, gx_send, gx_recv,
-           sf_send, sf_recv, sn_send, sn_recv, sx_send, sx_recv):
+           near_out, near_in, far_out, far_in,
+           ld_sem, st_sem, gf_send, gf_recv, gn_send, gn_recv, sf_send, sf_recv, sn_send, sn_recv):
     fars = nz // 4
     last = 2 * fars
-    early = fars // 2
     n_keys = 256 * last + 128
     alen = ans_len[0]
     plen = prompt_len[0]
@@ -50,22 +48,23 @@
     side = 1 - 2 * (lax.axis_index("group") % 2)
     par = me // nz
     z = me % nz
-    cross = {"ans": (1 - par) * nz + z}
 
     def along(step):
         return (z + side * step + 4 * nz) & (nz - 1)
 
-    places = {step: par * nz + along(step) for step in range(nz)}
-
-    def peer(step):
-        return {"ans": places[step % nz] if isinstance(step, int) else par * nz + along(step)}
-
+    places = {step: along(step) for step in range(nz)}
+
+    def peer(step, k=0):
+        there = places[step % nz] if isinstance(step, int) else along(step)
+        return {"ans": (1 - par if k else par) * nz + there}
+
+    far_steps = set()
+    for f in range(1, fars):
+        far_steps |= {far_step(f) % nz, -far_step(f) % nz}
+    others = [peer(step) for step in sorted(far_steps | {n % nz for n in (1, -1, 2, -2)})]
+    others += [peer(step, 1) for step in sorted(far_steps | {0})]
     barrier = pltpu.get_barrier_semaphore()
-    steps = {n % nz for n in (1, -1, 2, -2)}
-    for f in range(1, fars):
-        steps |= {far_step(f) % nz, -far_step(f) % nz}
-    steps = sorted(steps)
-    for other in [peer(step) for step in steps] + [cross]:
+    for other in others:
         pl.semaphore_signal(barrier, inc=1, device_id=other, device_id_type=MESH)
 
     loads = [pltpu.make_async_copy(kv_p, kv.at[0], ld_sem.at[2])]
@@ -81,48 +80,25 @@
         pltpu.make_async_copy(g_a.at[:, cols], g.at[pl.ds(h * ALEN, ALEN)], ld_sem.at[1]).start()
         pltpu.make_async_copy(g_p.at[:, cols], g.at[pl.ds(A_ROWS + h * PIECE, PIECE)], ld_sem.at[1]).start()
 
-    pl.semaphore_wait(barrier, len(steps) + 1)
+    pl.semaphore_wait(barrier, len(others))
 
     def remote(src, dst, send, recv, device):
         return pltpu.make_async_remote_copy(
             src_ref=src, dst_ref=dst, send_sem=send, recv_sem=recv,
             device_id=device, device_id_type=MESH)
 
-    def to_far(f):
-        return remote(kv_p, kv.at[8 * f], gf_send.at[f], gf_recv.at[f], peer(far_step(f)))
-
-    def to_near(f, k, n, src=None):
-        return remote(kv.at[8 * f + 4 * k] if src is None else src, kv.at[8 * f + 4 * k + n],
-                      gn_send.at[f, k, n], gn_recv.at[f, k, n], peer(near_step(f, n)))
-
-    def to_cross(f, n, src=None):
-        return remote(kv.at[8 * f + n] if src is None else src, kv.at[8 * f + 4 + n],
-                      gx_send.at[f, n], gx_recv.at[f, n], cross)
-
-    def spread_cross(f):
-        to_cross(f, 0).wait_recv()
-        for n in range(1, 4):
-            to_near(f, 1, n).start()
-
-    def near_arrived(f, k):
-        for n in range(1, 4):
-            to_near(f, k, n).wait_recv()
-
-    def near_to_cross(f):
-        for n in range(1, 4):
-            to_near(f, 0, n).wait_recv()
-            to_cross(f, n).start()
-
-    def cross_arrived(f):
-        for n in range(4):
-            to_cross(f, n).wait_recv()
+    far_pairs = [(0, 1)] + [(f, k) for f in range(1, fars) for k in range(2)]
+
+    def to_far(f, k):
+        return remote(kv_p, kv.at[8 * f + k], gf_send.at[f, k], gf_recv.at[f, k], peer(far_step(f), k))
+
+    def to_near(f, n):
+        return remote(kv.at[pl.ds(8 * f, 2)], kv.at[pl.ds(8 * f + 2 * n, 2)],
+                      gn_send.at[f, n], gn_recv.at[f, n], peer(near_step(f, n)))
 
     K, V = 0, 1
-    for f in range(1, fars):
-        to_far(f).start()
-    to_cross(0, 0, kv_p).start()
-    for n in range(1, 4):
-        to_near(0, 0, n, kv_p).start()
+    for f, k in far_pairs:
+        to_far(f, k).start()
 
     pltpu.make_async_copy(q, q, ld_sem.at[0]).wait()
     pltpu.make_async_copy(g, g, ld_sem.at[1]).wait()
@@ -178,9 +154,9 @@
             e[rows, lanes] = ex.reshape(n, LANES)
             dp[rows, lanes] = lax.dot_general(values, g[lanes, :], NT, preferred_element_type=F32)
 
-    def bases(f, k):
-        half = par if k == 0 else 1 - par
-        return [(half * nz + along(-(near_step(f, n) + far_step(f)))) * PIECE for n in range(4)]
+    def bases(f, half):
+        there = [along(-(near_step(f, 2 * half + i) + far_step(f))) for i in range(2)]
+        return [((1 - par if k else par) * nz + there[i]) * PIECE for i in range(2) for k in range(2)]
 
     def loop(first, stop, *steps):
         def body(i, carry):
@@ -202,20 +178,21 @@
         score_group(2 * f + k, bases(f, k))
 
     score_group(last, [], True)
-    for f in range(1, fars):
-        to_far(f).wait_recv()
-        to_cross(f, 0).start()
+    for f in range(fars):
+        for k in range(2):
+            if (f, k) in far_pairs:
+                to_far(f, k).wait_recv()
         for n in range(1, 4):
-            to_near(f, 0, n).start()
-    for f in range(early):
-        spread_cross(f)
-        near_arrived(f, 0)
+            to_near(f, n).start()
+
+    def score_far(f):
+        to_near(f, 1).wait_recv()
         score(f, 0)
-    for f in range(early, fars):
-        near_to_cross(f)
-    loop(early, fars, lambda f: score(f, 0))
-    loop(0, early, lambda f: near_arrived(f, 1), lambda f: score(f, 1))
-    loop(early, fars, lambda f: cross_arrived(f), lambda f: score(f, 1))
+        to_near(f, 2).wait_recv()
+        to_near(f, 3).wait_recv()
+        score(f, 1)
+
+    loop(0, fars, score_far)
 
     m8 = mrun[...]
     top = jnp.max(m8, axis=0, keepdims=True)
@@ -250,113 +227,73 @@
         rows = jnp.dot(kt[...], ds[:, lanes], preferred_element_type=F32)
         dq[lanes, :] = rows.T.astype(BF16)
 
-    def sum_cross(c, f):
-        rows = pl.ds(0, 256 if f >= early else PIECE)
-        return remote(x_out.at[c, f, rows], x_in.at[c, f, rows], sx_send.at[c, f], sx_recv.at[c, f], cross)
-
-    def sum_near(c, f, k, n):
-        return remote(near_out.at[c, f, k, n - 1], near_in.at[c, f, k, n - 1],
-                      sn_send.at[c, f, k, n - 1], sn_recv.at[c, f, k, n - 1], peer(-near_step(f, n)))
-
-    def sum_far(c, f):
-        return remote(far_out.at[c, f - 1], far_in.at[c, f - 1],
-                      sf_send.at[c, f - 1], sf_recv.at[c, f - 1], peer(-far_step(f)))
-
-    def send_near(c, f, k):
-        if k == 0 and f >= early:
-            sum_cross(c, f).wait_recv()
-        row = 512 * f + 256 * k
+    def sum_near(c, f, n):
+        return remote(near_out.at[c, f, n - 1], near_in.at[c, f, n - 1],
+                      sn_send.at[c, f, n - 1], sn_recv.at[c, f, n - 1], peer(-near_step(f, n)))
+
+    def sum_far(c, f, k):
+        return remote(far_out.at[c, f, k], far_in.at[c, f, k],
+                      sf_send.at[c, f, k], sf_recv.at[c, f, k], peer(-far_step(f), k))
+
+    def send_near(c, f):
         for n in range(1, 4):
-            part = terms[c, row + n * PIECE:row + (n + 1) * PIECE, :]
-            if k == 0 and f >= early:
-                part = part + x_in[c, f, n * PIECE:(n + 1) * PIECE, :].astype(F32)
-            near_out[c, f, k, n - 1] = part.astype(BF16)
-            sum_near(c, f, k, n).start()
-
-    def near_sum(c, f, k):
-        row = 512 * f + 256 * k
-        acc = terms[c, row:row + PIECE, :]
+            row = pl.multiple_of(512 * f + 128 * n, 128)
+            near_out[c, f, n - 1] = terms[c, pl.ds(row, 128), :].astype(BF16)
+            sum_near(c, f, n).start()
+
+    def near_sum(c, f):
+        acc = terms[c, 512 * f:512 * f + 128, :]
         for n in range(1, 4):
-            sum_near(c, f, k, n).wait_recv()
-            acc = acc + near_in[c, f, k, n - 1].astype(F32)
+            sum_near(c, f, n).wait_recv()
+            acc = acc + near_in[c, f, n - 1].astype(F32)
         return acc
 
-    def send_cross(c, f):
-        if f >= early:
-            x_out[c, f] = terms[c, 512 * f + 256:512 * f + 512, :].astype(BF16)
-        else:
-            x_out[c, f, 0:PIECE] = near_sum(c, f, 1).astype(BF16)
-        sum_cross(c, f).start()
-
-    def held(c, f):
-        acc = near_sum(c, f, 0)
-        if f < early:
-            sum_cross(c, f).wait_recv()
-        return acc + x_in[c, f, 0:PIECE, :].astype(F32)
-
     def send_far(c, f):
-        far_out[c, f - 1] = held(c, f).astype(BF16)
-        sum_far(c, f).start()
+        acc = near_sum(c, f)
+        for k in range(2):
+            if (f, k) in far_pairs:
+                far_out[c, f, k] = acc[k * PIECE:(k + 1) * PIECE].astype(BF16)
+                sum_far(c, f, k).start()
+        if f == 0:
+            terms[c, 0:PIECE, :] = acc[0:PIECE]
 
     def finish(c):
-        acc = held(c, 0)
-        for f in range(1, fars):
-            sum_far(c, f).wait_recv()
-            acc = acc + far_in[c, f - 1].astype(F32)
+        acc = terms[c, 0:PIECE, :]
+        for f, k in far_pairs:
+            sum_far(c, f, k).wait_recv()
+            acc = acc + far_in[c, f, k].astype(F32)
         prm_out[c] = acc.astype(BF16)
 
-    late_groups = list(range(fars - 1, early - 1, -1))
-    early_groups = list(range(early - 1, -1, -1))
-    far_groups = list(range(fars - 1, 0, -1))
-
-    for f in late_groups:
-        value_terms(2 * f + 1)
-        send_cross(V, f)
-    for f in early_groups:
-        value_terms(2 * f + 1)
-        send_near(V, f, 1)
-    for f in early_groups:
-        value_terms(2 * f)
-        send_near(V, f, 0)
-    loop(fars, early, lambda f: value_terms(2 * f))
+    def terms_of(c, fn):
+        def both(f):
+            fn(2 * f)
+            fn(2 * f + 1)
+            send_near(c, f)
+        return both
+
+    loop(fars, 0, terms_of(V, value_terms))
     value_terms(last, 128)
     delta[...] = jnp.broadcast_to(jnp.sum(delta[...], axis=0, keepdims=True), delta.shape)
-    for f in late_groups:
-        key_terms(2 * f + 1)
-        send_cross(K, f)
-    for f in late_groups:
-        send_near(V, f, 0)
-    for f in early_groups:
-        key_terms(2 * f + 1)
-        send_near(K, f, 1)
-    for f in early_groups:
-        send_cross(V, f)
-    for f in early_groups:
-        key_terms(2 * f)
-        send_near(K, f, 0)
-    loop(fars, early, lambda f: key_terms(2 * f))
-    for f in late_groups:
-        send_near(K, f, 0)
+    loop(fars, fars // 2, terms_of(K, key_terms))
+    for f in range(fars - 1, fars // 2 - 1, -1):
+        send_far(V, f)
+    loop(fars // 2, 0, terms_of(K, key_terms))
+    for f in range(fars // 2 - 1, -1, -1):
+        send_far(V, f)
     key_terms(last, 128)
     own_out[...] = terms[:, 256 * last:256 * last + ALEN, :].astype(BF16)
     own_store = pltpu.make_async_copy(own_out, dkv_a, st_sem.at[0])
     own_store.start()
-    for f in far_groups:
-        send_far(V, f)
-    for f in early_groups:
-        send_cross(K, f)
     for s in range(n_keys // 128):
         kt[:, s * 128:(s + 1) * 128] = kv[2 * s:2 * s + 2, 0].reshape(128, HD).T
     for j in range(CHUNKS // 2):
         query_terms(j)
-    late_far = [f for f in far_groups if f >= early]
-    for f in late_far:
+    for f in range(fars - 1, fars // 2 - 1, -1):
         send_far(K, f)
     for j in range(CHUNKS // 2, CHUNKS):
         query_terms(j)
-    for f in far_groups:
-        if f not in late_far:
-            send_far(K, f)
+    for f in range(fars // 2 - 1, -1, -1):
+        send_far(K, f)
     for h in range(HEADS):
         cols = pl.ds(h * HD, HD)
         pltpu.make_async_copy(dq.at[pl.ds(h * ALEN, ALEN)], dq_a.at[:, cols], st_sem.at[1]).start()
@@ -364,22 +301,17 @@
 
     def sent(c):
         for f in range(fars):
-            for k in range(1 if f >= early else 2):
-                for n in range(1, 4):
-                    sum_near(c, f, k, n).wait_send()
-            sum_cross(c, f).wait_send()
-            if f:
-                sum_far(c, f).wait_send()
-
+            for n in range(1, 4):
+                sum_near(c, f, n).wait_send()
+        for f, k in far_pairs:
+            sum_far(c, f, k).wait_send()
+
+    for f in range(fars):
+        for n in range(1, 4):
+            to_near(f, n).wait_send()
+    for f, k in far_pairs:
+        to_far(f, k).wait_send()
     finish(V)
-    for f in range(fars):
-        for n in range(4 if f >= early else 1):
-            to_cross(f, n).wait_send()
-        for k in range(1 if f >= early else 2):
-            for n in range(1, 4):
-                to_near(f, k, n).wait_send()
-        if f:
-            to_far(f).wait_send()
     sent(V)
     own_store.wait()
     pltpu.make_async_copy(dq, dq, st_sem.at[1]).wait()
@@ -434,14 +366,11 @@
             vm((ROWS, HD), BF16),
             vm((2, ALEN, HD), BF16),
             vm((2, PIECE, HD), BF16),
-            vm((2, fars, 256, HD), BF16), vm((2, fars, 256, HD), BF16),
-            vm((2, fars, 2, 3, PIECE, HD), BF16), vm((2, fars, 2, 3, PIECE, HD), BF16),
-            vm((2, fars - 1, PIECE, HD), BF16), vm((2, fars - 1, PIECE, HD), BF16),
+            vm((2, fars, 3, 2 * PIECE, HD), BF16), vm((2, fars, 3, 2 * PIECE, HD), BF16),
+            vm((2, fars, 2, PIECE, HD), BF16), vm((2, fars, 2, PIECE, HD), BF16),
             dma((5,)), dma((3,)),
-            dma((fars,)), dma((fars,)), dma((fars, 2, 4)), dma((fars, 2, 4)),
-            dma((fars, 4)), dma((fars, 4)),
-            dma((2, fars - 1)), dma((2, fars - 1)), dma((2, fars, 2, 3)), dma((2, fars, 2, 3)),
-            dma((2, fars)), dma((2, fars)),
+            dma((fars, 2)), dma((fars, 2)), dma((fars, 4)), dma((fars, 4)),
+            dma((2, fars, 2)), dma((2, fars, 2)), dma((2, fars, 3)), dma((2, fars, 3)),
         ],
         compiler_params=pltpu.CompilerParams(
             collective_id=0, has_side_effects=True, vmem_limit_bytes=58 * 1024 * 1024),

time: 63 us -> 75.1 us (1.19)
  Pallas kernels: 60.9 us -> 72.5 us
    pallas_call x1, Pallas kernels: 59.1 us -> 70.7 us  [per_device(): pl.pallas_call(functools.partial(kernel, nz), out_shape=out_shape, in_spe...]
where the time goes in v8:
time: 75.1 us; the launch traced here: 74.4 us
  Pallas kernels  72.5 us (97%)
  between operations  1.93 us (3%)
    pallas_call x1, Pallas kernels, per_device(): pl.pallas_call(functools.partial(kernel, nz), out_shape=out_shape, in_spe...  70.7 us
    pallas_call x1, Pallas kernels, per_device(): pl.pallas_call(deliver, out_shape=out_shape, in_specs=[any_spec] * 4, out...  1.79 us

profile of v8, /device:TPU:24, one launch (start us, length us, event | category | flops | bytes accessed | tf_op | source)
XLA Modules:
  0.0 74.4 jit_solution(6895365558700741652)
XLA Ops:
  1.9 70.7 %shard_map.111 = (bf16[128,1024]{1,0:T(8,128)(2,1)}, bf16[2,128,128]{2,1,0:T(8,128)(2,1)}, bf16[64,1024]{1,0:T(8,128)(2,1)}, bf16[2,64,128]{2,1,0:T(8,128)(2,1)}) custom-call(s32[1]{0:T(128)S(6)} %copy.12.ans_len, s32[1]{0:T(128)S(6)} %copy.13.prompt_len, bf16[128,1024]{1,0:T(8,128)(2,1)} %q_a.1, bf16[2,128,128]{2,1,0:T(8,128)(2,1)} %kv_a.1, ...), custom_call_target="tpu_custom_call" | custom-call | tf_op jit(solution)/shard_map/pallas_call | solution.py:346
  72.6 1.8 %shard_map.112 = (bf16[128,1024]{1,0:T(8,128)(2,1)}, bf16[2,128,128]{2,1,0:T(8,128)(2,1)}, bf16[64,1024]{1,0:T(8,128)(2,1)}, bf16[2,64,128]{2,1,0:T(8,128)(2,1)}) custom-call(bf16[128,1024]{1,0:T(8,128)(2,1)} %get-tuple-element.8.refs_0_, bf16[2,128,128]{2,1,0:T(8,128)(2,1)} %get-tuple-element.9.refs_1_, bf16[64,1024]{1,0:T(8,128)(2,1)} %get-tuple-element.10.refs_2_, ...), custom_call_target="tpu_custom_call" | custom-call | tf_op jit(solution)/shard_map/pallas_call | solution.py:378

commit v9 on v7

--- a/solution.py
+++ b/solution.py
@@ -25,12 +25,16 @@
 NT = (((1,), (1,)), ((), ()))
 
 
+def leans(f):
+    return (f + 1) // 2 % 2
+
+
 def far_step(f):
-    return 4 * f + f % 2
+    return 4 * f + leans(f)
 
 
 def near_step(f, n):
-    return (0, 1, -1, 2 - 4 * (f % 2))[n]
+    return (0, 1, -1, 2 - 4 * leans(f))[n]
 
 
 def kernel(nz, ans_len, prompt_len, q_a, kv_a, q_p, kv_p, g_a, g_p,
@@ -42,7 +46,7 @@
            sf_send, sf_recv, sn_send, sn_recv, sx_send, sx_recv):
     fars = nz // 4
     last = 2 * fars
-    early = fars // 2
+    early = max(1, fars // 4)
     n_keys = 256 * last + 128
     alen = ans_len[0]
     plen = prompt_len[0]
@@ -349,7 +353,7 @@
         kt[:, s * 128:(s + 1) * 128] = kv[2 * s:2 * s + 2, 0].reshape(128, HD).T
     for j in range(CHUNKS // 2):
         query_terms(j)
-    late_far = [f for f in far_groups if f >= early]
+    late_far = far_groups[:1]
     for f in late_far:
         send_far(K, f)
     for j in range(CHUNKS // 2, CHUNKS):

time: 63 us -> 63.1 us (level)
  no operation moved by 1% of the time
where the time goes in v9:
time: 63.1 us; the launch traced here: 62.9 us
  Pallas kernels  61 us (97%)
  between operations  1.93 us (3%)
    pallas_call x1, Pallas kernels, per_device(): pl.pallas_call(functools.partial(kernel, nz), out_shape=out_shape, in_spe...  59.2 us
    pallas_call x1, Pallas kernels, per_device(): pl.pallas_call(deliver, out_shape=out_shape, in_specs=[any_spec] * 4, out...  1.79 us

profile of v9, /device:TPU:24, one launch (start us, length us, event | category | flops | bytes accessed | tf_op | source)
XLA Modules:
  0.0 62.9 jit_solution(14831866099304288165)
XLA Ops:
  1.9 59.2 %shard_map.111 = (bf16[128,1024]{1,0:T(8,128)(2,1)}, bf16[2,128,128]{2,1,0:T(8,128)(2,1)}, bf16[64,1024]{1,0:T(8,128)(2,1)}, bf16[2,64,128]{2,1,0:T(8,128)(2,1)}) custom-call(s32[1]{0:T(128)S(6)} %copy.12.ans_len, s32[1]{0:T(128)S(6)} %copy.13.prompt_len, bf16[128,1024]{1,0:T(8,128)(2,1)} %q_a.1, bf16[2,128,128]{2,1,0:T(8,128)(2,1)} %kv_a.1, ...), custom_call_target="tpu_custom_call" | custom-call | tf_op jit(solution)/shard_map/pallas_call | solution.py:418
  61.1 1.8 %shard_map.112 = (bf16[128,1024]{1,0:T(8,128)(2,1)}, bf16[2,128,128]{2,1,0:T(8,128)(2,1)}, bf16[64,1024]{1,0:T(8,128)(2,1)}, bf16[2,64,128]{2,1,0:T(8,128)(2,1)}) custom-call(bf16[128,1024]{1,0:T(8,128)(2,1)} %get-tuple-element.8.refs_0_, bf16[2,128,128]{2,1,0:T(8,128)(2,1)} %get-tuple-element.9.refs_1_, bf16[64,1024]{1,0:T(8,128)(2,1)} %get-tuple-element.10.refs_2_, ...), custom_call_target="tpu_custom_call" | custom-call | tf_op jit(solution)/shard_map/pallas_call | solution.py:453
